TPU v7x, 32 devices: a whole 2x2x4 slice. The times are simulated.
32 devices in a mesh: seq: 8 (over y, x, core), vis: 4 (over z).
Axes of the slice: x: 2, y: 2, z: 4, core: 2. Of those that a mesh axis runs over, the one named last changes fastest.
Arguments:
- text: bfloat16 [2048, 8192], P('seq'), may hold values from -6 to 6
- frames: bfloat16 [2048, 8192], P(('seq', 'vis')), may hold values from -60 to 60
- tile_pos: int32 [2048], P(('seq', 'vis')), may hold values from 0 to 2047, as said below
- frame_count: int32 [32], P(('seq', 'vis')), may hold values from 8 to 64
- doc_ids: int32 [2048], replicated, may hold values from 0 to 3, never falling along the last dimension, each value on 1 to 1024 neighbouring positions
- norm_gain: float32 [8192], replicated, may hold values from 0.1 to 1.9
- w_query: bfloat16 [8192, 8192], P(None, 'vis'), may hold values from -4 to 4
- q_bias: float32 [8192], P('vis'), may hold values from -3 to 3
- w_key: bfloat16 [8192, 1024], P(None, 'vis'), may hold values from -4 to 4
- w_value: bfloat16 [8192, 1024], P(None, 'vis'), may hold values from -0.0625 to 0.0625
- v_bias: float32 [1024], P('vis'), may hold values from -3 to 3
Outputs:
- attended: bfloat16 [2048, 8192], P('seq', 'vis')
Inputs may be any that keep to these rules, and one draw needn't show every extreme that they name: `tile_pos`: all entries together name every position of the window once. Of one device's 64 rows, at most 8 of those below its frame_count fall into one shard of 256 positions, and in every draw one shard receives exactly 8 usable rows from every device. Rows at or beyond the count are unused. `doc_ids`: never falling along the window.
All inputs are finite; a program needn't handle non-finite values.
Results may differ from a plain program's by a relative error of at most 0.0069.
Values may be sent and summed in bfloat16 or wider, within the bound.
No kernel may reach another device: no remote copies, remote signals or barrier semaphores. Data moves between devices by JAX's collectives and lax.ppermute only.
A program may use at most 128 MiB of HBM per device.

v0:
```python
import functools

import jax
import jax.numpy as jnp
from jax import lax
from jax.experimental import pallas as pl
from jax.experimental.pallas import tpu as pltpu
from jax.sharding import PartitionSpec as P

HEAD_DIM = 128
META = 128
CHUNKS = 4
EPSILON = 1e-06
NEGATIVE = -1e30
LOG2_E = 1.4426950408889634
VMEM_LIMIT = 48 * 1024 * 1024
F32 = jnp.float32
BF16 = jnp.bfloat16


def params(limit=VMEM_LIMIT):
    return pltpu.CompilerParams(vmem_limit_bytes=limit)


def cost(flops, moved):
    return pl.CostEstimate(flops=int(flops), bytes_accessed=int(moved), transcendentals=0)


def normed_rows(rows, gain):
    widened = rows.astype(F32)
    mean_square = jnp.mean(widened * widened, axis=1, keepdims=True)
    return (widened * lax.rsqrt(mean_square + EPSILON) * gain).astype(BF16)


def slots_kernel(scalars, frames, gain, place_row, out, *, shard_rows, capacity):
    count, shard = scalars[0], scalars[1]
    rows, width = frames.shape
    across = lax.broadcasted_iota(jnp.int32, (rows, rows), 1)
    down = lax.broadcasted_iota(jnp.int32, (rows, rows), 0)
    places = jnp.broadcast_to(place_row[...], (rows, rows))
    place_column = jnp.sum(jnp.where(down == across, places, 0), axis=1, keepdims=True)
    owner_row = place_row[...] // shard_rows
    owner_column = place_column // shard_rows
    same = (owner_row == owner_column) & (down < across) & (down < count)
    rank = jnp.sum(same.astype(jnp.int32), axis=0, keepdims=True)
    slot = (owner_row ^ shard) * capacity + rank
    pick = ((slot == down) & (across < count)).astype(BF16)
    local = place_column - owner_column * shard_rows + 1
    tags = jnp.broadcast_to(local.astype(F32), (rows, META)).astype(BF16)
    normed = normed_rows(frames[...], gain[...])
    lead = (out.shape[1] - META) // CHUNKS
    out[:, :lead] = jnp.dot(pick, normed[:, :lead], preferred_element_type=F32).astype(BF16)
    out[:, lead : lead + META] = jnp.dot(pick, tags, preferred_element_type=F32).astype(BF16)
    out[:, lead + META :] = jnp.dot(pick, normed[:, lead:], preferred_element_type=F32).astype(BF16)


def make_slots(frames, gain, tile_pos, frame_count, shard, shard_rows, capacity):
    rows, width = frames.shape
    scalars = jnp.stack([frame_count[0], shard.astype(jnp.int32)])
    return pl.pallas_call(
        functools.partial(slots_kernel, shard_rows=shard_rows, capacity=capacity),
        out_shape=jax.ShapeDtypeStruct((rows, width + META), BF16),
        in_specs=[pl.BlockSpec(memory_space=pltpu.SMEM)]
        + [pl.BlockSpec(memory_space=pltpu.VMEM)] * 3,
        out_specs=pl.BlockSpec(memory_space=pltpu.VMEM),
        compiler_params=params(),
        cost_estimate=cost(2 * rows * rows * width, 4 * rows * width),
        name="frame_slots",
    )(scalars, frames, gain.reshape(1, width), tile_pos.reshape(1, rows))


def scale_kernel(rows, out):
    widened = rows[...].astype(F32)
    mean_square = jnp.mean(widened * widened, axis=1, keepdims=True)
    out[...] = jnp.broadcast_to(lax.rsqrt(mean_square + EPSILON), out.shape)


def text_scale(text):
    rows, width = text.shape
    step = 64
    return pl.pallas_call(
        scale_kernel,
        out_shape=jax.ShapeDtypeStruct((rows, META), F32),
        grid=(rows // step,),
        in_specs=[pl.BlockSpec((step, width), lambda i: (i, 0))],
        out_specs=pl.BlockSpec((step, META), lambda i: (i, 0)),
        compiler_params=params(),
        cost_estimate=cost(3 * rows * width, 2 * rows * width),
        name="text_scale",
    )(text)


def assemble_kernel(*refs, parts):
    at = 0
    for out in refs[parts:]:
        end = at + out.shape[1]
        found = [ref[:, at:end].astype(F32) for ref in refs[:parts]]
        out[...] = jnp.concatenate(found, axis=0).astype(BF16)
        at = end


def assemble(parts, widths):
    rows = sum(part.shape[0] for part in parts)
    if parts[0].shape[0] % 8:
        whole = jnp.concatenate(parts)
        cuts = [sum(widths[:i]) for i in range(len(widths) + 1)]
        return [whole[:, a:b] for a, b in zip(cuts, cuts[1:])]
    vmem = pl.BlockSpec(memory_space=pltpu.VMEM)
    return pl.pallas_call(
        functools.partial(assemble_kernel, parts=len(parts)),
        out_shape=[jax.ShapeDtypeStruct((rows, width), BF16) for width in widths],
        in_specs=[vmem] * len(parts),
        out_specs=[vmem] * len(widths),
        compiler_params=params(),
        cost_estimate=cost(rows * sum(widths), 4 * rows * sum(widths)),
        name="assemble",
    )(*parts)


def after(value, *earlier):
    return lax.optimization_barrier((value, earlier))[0]


def swap_slots(block, count, capacity):
    parts = [block[:capacity]]
    for d in range(1, count):
        sent = block[d * capacity : (d + 1) * capacity]
        parts.append(lax.ppermute(sent, "seq", [(i, i ^ d) for i in range(count)]))
    return parts


def hop_pairs(count, s, odd):
    links = range(odd, count - 1, 2)
    up = [(i, i + 1) for i in links if i >= s - 1]
    return up + [(i + 1, i) for i in links if i + 1 <= count - s]


def merge_kernel(*refs, blocks, rows, fresh, finish):
    tags, incoming = refs[:blocks], refs[blocks : 2 * blocks]
    text, scale, gain, w_key, w_value = refs[2 * blocks : 2 * blocks + 5]
    merged, keyval = refs[-5], refs[-4]
    total, pick, covered = refs[-3:]
    step = pl.program_id(0)
    slots = tags[0].shape[0]
    half = w_key.shape[1]

    @pl.when(step == 0)
    def _():
        places = jnp.concatenate([ref[...] for ref in tags], axis=0).astype(F32).T[:1, :]
        wanted = lax.broadcasted_iota(jnp.int32, (rows, blocks * slots), 0) + 1
        chosen = (places.astype(jnp.int32) == wanted).astype(F32)
        pick[...] = chosen.astype(BF16)
        covered[...] = jnp.broadcast_to(jnp.sum(chosen, axis=1, keepdims=True), covered.shape)
        total[...] = jnp.zeros_like(total) if fresh else refs[2 * blocks + 5][...]

    found = jnp.concatenate([ref[...] for ref in incoming], axis=0)
    placed = jnp.dot(pick[...], found, preferred_element_type=F32)
    normed = text[...].astype(F32) * scale[:, :1] * gain[...]
    rows_here = jnp.where(covered[:, :1] > 0.5, placed, normed).astype(BF16)
    merged[...] = rows_here
    total[:, :half] += jnp.dot(rows_here, w_key[...], preferred_element_type=F32)
    total[:, half:] += jnp.dot(rows_here, w_value[...], preferred_element_type=F32)

    @pl.when(step == pl.num_programs(0) - 1)
    def _():
        if finish:
            v_bias = refs[2 * blocks + 6]
            keyval[:, :half] = total[:, :half].astype(BF16)
            keyval[:, half:] = (total[:, half:] + v_bias[...]).astype(BF16)
        else:
            keyval[...] = total[...]


def merge_chunk(
    tags, incoming, text, scale, gain, w_key, w_value, total, first, width, v_bias, earlier
):
    blocks, slots = len(tags), tags[0].shape[0]
    rows = text.shape[0]
    step = 1024
    lead_step = first // step
    tag_column = width // META
    cols = w_key.shape[1]
    fresh, finish = total is None, v_bias is not None
    whole = pl.BlockSpec((rows, 2 * cols), lambda i: (0, 0))
    extra = [] if fresh else [total]
    extra_specs = [] if fresh else [whole]
    if finish:
        extra.append(v_bias.reshape(1, cols))
        extra_specs.append(pl.BlockSpec((1, cols), lambda i: (0, 0)))
    extra += earlier
    extra_specs += [pl.BlockSpec(memory_space=pl.ANY)] * len(earlier)
    return pl.pallas_call(
        functools.partial(merge_kernel, blocks=blocks, rows=rows, fresh=fresh, finish=finish),
        out_shape=(
            jax.ShapeDtypeStruct((rows, width), BF16),
            jax.ShapeDtypeStruct((rows, 2 * cols), BF16 if finish else F32),
        ),
        grid=(width // step,),
        in_specs=[pl.BlockSpec((slots, META), lambda i: (0, tag_column))] * blocks
        + [pl.BlockSpec((slots, step), lambda i: (0, i))] * blocks
        + [
            pl.BlockSpec((rows, step), lambda i: (0, i + lead_step)),
            pl.BlockSpec((rows, META), lambda i: (0, 0)),
            pl.BlockSpec((1, step), lambda i: (0, i + lead_step)),
            pl.BlockSpec((step, cols), lambda i: (i + lead_step, 0)),
            pl.BlockSpec((step, cols), lambda i: (i + lead_step, 0)),
        ]
        + extra_specs,
        out_specs=(pl.BlockSpec((rows, step), lambda i: (0, i)), whole),
        scratch_shapes=[
            pltpu.VMEM((rows, 2 * cols), F32),
            pltpu.VMEM((rows, blocks * slots), BF16),
            pltpu.VMEM((rows, META), F32),
        ],
        compiler_params=params(),
        cost_estimate=cost(
            2 * rows * width * (2 * cols + blocks * slots),
            2 * width * (blocks * slots + 2 * rows + 2 * cols),
        ),
        name="merge_rows",
    )(*tags, *incoming, text, scale, gain.reshape(1, -1), w_key, w_value, *extra)


def query_kernel(*refs, parts, finish):
    rows, (weights, bias, out) = refs[:parts], refs[parts:]
    total = bias[...]
    depth = rows[0].shape[1]
    for p in range(parts):
        total = total + jnp.dot(
            rows[p][...], weights[p * depth : (p + 1) * depth, :], preferred_element_type=F32
        )
    if finish:
        count = total.shape[0]
        for j in range(total.shape[1] // HEAD_DIM):
            head = total[:, j * HEAD_DIM : (j + 1) * HEAD_DIM]
            out[0, :, j * count : (j + 1) * count] = head.T.astype(BF16)
    else:
        out[...] = total


def project_queries(parts, weights, first, earlier, groups):
    rows, depth = parts[0].shape
    cols = weights.shape[1]
    taken = depth * len(parts)
    step = 512
    out_shape = jax.ShapeDtypeStruct((rows, cols), F32)
    out_spec = pl.BlockSpec((rows, step), lambda i: (0, i))
    if groups:
        wide = cols // groups // HEAD_DIM * rows
        share = cols // groups // step
        out_shape = jax.ShapeDtypeStruct((groups, HEAD_DIM, wide), BF16)
        out_spec = pl.BlockSpec((1, HEAD_DIM, wide // share), lambda i: (i // share, 0, i % share))
    return pl.pallas_call(
        functools.partial(query_kernel, parts=len(parts), finish=groups > 0),
        out_shape=out_shape,
        grid=(cols // step,),
        in_specs=[pl.BlockSpec((rows, depth), lambda i: (0, 0))] * len(parts)
        + [
            pl.BlockSpec((taken, step), lambda i: (first // taken, i)),
            pl.BlockSpec((earlier.shape[0], step), lambda i: (0, i)),
        ],
        out_specs=out_spec,
        compiler_params=params(),
        cost_estimate=cost(2 * rows * taken * cols, 2 * (rows + cols) * taken),
        name="queries",
    )(*parts, weights, earlier)


def attend_kernel(*refs, blocks, kv_heads, resume, finish):
    needed, queries, docs_row, docs_column, places = refs[:5]
    keyvals = refs[5 : 5 + blocks]
    rest = refs[5 + blocks :]
    earlier, rest = (rest[:3], rest[3:]) if resume else (None, rest)
    out, (peak, total, summed) = (rest[0], rest[1:]) if finish else (None, rest)
    rows = docs_row.shape[1]
    wide = queries.shape[2]
    span = 8 * rows
    scale = HEAD_DIM ** (-0.5) * LOG2_E
    if resume:
        peak[...] = earlier[0][...]
        total[...] = earlier[1][...]
        summed[...] = earlier[2][...]
    else:
        peak[...] = jnp.full_like(peak, NEGATIVE)
        total[...] = jnp.zeros_like(total)
        summed[...] = jnp.zeros_like(summed)
    key_width = kv_heads * HEAD_DIM

    def one_block(b):
        down = lax.broadcasted_iota(jnp.int32, (rows, rows), 0)
        across = lax.broadcasted_iota(jnp.int32, (rows, rows), 1)
        allowed = (down - places[b] <= across) & (docs_column[b] == docs_row[...])
        bias = jnp.where(allowed, 0.0, NEGATIVE)
        bias = jnp.concatenate([bias] * (span // rows), axis=1)
        for g in range(kv_heads):
            keys = keyvals[b][:, g * HEAD_DIM : (g + 1) * HEAD_DIM]
            values = keyvals[b][:, key_width + g * HEAD_DIM : key_width + (g + 1) * HEAD_DIM].T
            for at in range(0, wide, span):
                part = slice(at, at + span)
                scores = jnp.dot(keys, queries[g, :, part], preferred_element_type=F32)
                scores = scores * scale + bias
                old = peak[g, :, part]
                new = jnp.maximum(old, jnp.max(scores, axis=0, keepdims=True))
                raised = jnp.exp2(scores - new)
                factor = jnp.exp2(old - new)
                peak[g, :, part] = new
                total[g, :, part] = total[g, :, part] * factor + jnp.sum(
                    raised, axis=0, keepdims=True
                )
                product = jnp.dot(values, raised.astype(BF16), preferred_element_type=F32)
                summed[g, :, part] = summed[g, :, part] * factor + product

    for b in range(blocks):
        pl.when(needed[b] > 0)(functools.partial(one_block, b))
    if finish:
        for g in range(kv_heads):
            for j in range(wide // rows):
                part = slice(j * rows, (j + 1) * rows)
                result = (summed[g, :, part] * (1.0 / total[g, :, part])).T
                at = (g * (wide // rows) + j) * HEAD_DIM
                out[:, at : at + HEAD_DIM] = result.astype(BF16)


def attend(needed, queries, docs_row, docs_columns, places, keyvals, state, finish, kv_heads):
    wide = queries.shape[2]
    rows = docs_row.shape[1]
    cols = kv_heads * wide // rows * HEAD_DIM
    state_shapes = ((kv_heads, 1, wide), (kv_heads, 1, wide), (kv_heads, HEAD_DIM, wide))
    vmem = pl.BlockSpec(memory_space=pltpu.VMEM)
    smem = pl.BlockSpec(memory_space=pltpu.SMEM)
    blocks = len(keyvals)
    out_shape = (
        jax.ShapeDtypeStruct((rows, cols), BF16)
        if finish
        else tuple(jax.ShapeDtypeStruct(s, F32) for s in state_shapes)
    )
    return pl.pallas_call(
        functools.partial(
            attend_kernel,
            blocks=blocks,
            kv_heads=kv_heads,
            resume=state is not None,
            finish=finish,
        ),
        out_shape=out_shape,
        in_specs=[smem, vmem, vmem, vmem, smem] + [vmem] * (blocks + (3 if state else 0)),
        out_specs=vmem if finish else (vmem,) * 3,
        scratch_shapes=[pltpu.VMEM(s, F32) for s in state_shapes] if finish else [],
        compiler_params=params(),
        cost_estimate=cost(4 * rows * rows * cols * blocks, 4 * rows * cols),
        name="attend_rest" if finish else "attend_own",
    )(needed, queries, docs_row, docs_columns, places, *keyvals, *(state or ()))


def on_device(
    text, frames, tile_pos, frame_count, doc_ids, norm_gain, w_query, q_bias, w_key, w_value, v_bias
):
    seq_count = lax.axis_size("seq")
    vis_count = lax.axis_size("vis")
    shard = lax.axis_index("seq")
    rows, width = text.shape
    capacity = rows // (seq_count * vis_count)
    kv_heads = w_key.shape[1] // HEAD_DIM

    chunk = width // CHUNKS
    slots = make_slots(frames, norm_gain, tile_pos, frame_count, shard, rows, capacity)
    parts = swap_slots(slots, seq_count, capacity)
    pieces = assemble(parts, [chunk + META] + [chunk] * (CHUNKS - 1))
    scale = text_scale(after(text, pieces[0]))
    found = [{} for _ in pieces]
    merged, sums = [], {"total": None, "queries": q_bias.reshape(1, -1)}

    def hop(c, s, *earlier):
        for odd in (0, 1):
            pairs = hop_pairs(vis_count, s, odd)
            if pairs:
                sent = pieces[c] if s == 1 else found[c][(s - 1, 1 - odd)]
                if earlier:
                    sent = after(sent, *earlier)
                found[c][(s, odd)] = lax.ppermute(sent, "vis", pairs)
        return [found[c][(s, odd)] for odd in (0, 1) if (s, odd) in found[c]]

    def merge(c, *earlier):
        part, sums["total"] = merge_chunk(
            [pieces[0], *found[0].values()],
            [pieces[c], *found[c].values()],
            text,
            scale,
            norm_gain,
            w_key,
            w_value,
            sums["total"],
            c * chunk,
            chunk,
            v_bias if c == CHUNKS - 1 else None,
            list(earlier),
        )
        merged.append(part)

    def query(c):
        sums["queries"] = project_queries([merged[c]], w_query, c * chunk, sums["queries"], 0)

    for s in range(1, vis_count):
        for c in range(CHUNKS):
            hop(c, s)
    for c in range(CHUNKS):
        if c == 2:
            query(0)
            query(1)
        merge(c, *([sums["queries"]] if c == 2 else []))
    keyval = sums["total"]

    half = CHUNKS // 2
    queries = project_queries(
        merged[half:], w_query, half * chunk, sums["queries"], kv_heads
    )

    chips = seq_count // 2
    near, others = [(keyval, shard)], []
    for mask in range(1, chips):
        pairs = [(c, c ^ mask) for c in range(chips) if 0 < (c ^ mask) - c <= chips // 2]
        pairs = [(2 * a + core, 2 * b + core) for a, b in pairs for core in (0, 1)]
        near.append((lax.ppermute(keyval, "seq", pairs), shard ^ (2 * mask)))
    docs = doc_ids.reshape(seq_count, rows)
    docs_row = lax.dynamic_slice_in_dim(docs, shard, 1)
    docs_own = docs_row.reshape(1, rows, 1)
    one = jnp.ones((1,), jnp.int32)
    state = attend(
        one, queries, docs_row, docs_own, 0 * one, [keyval], None, False, kv_heads
    )
    core_swap = [(i, i ^ 1) for i in range(seq_count)]
    for held, origin in near:
        others.append((lax.ppermute(after(held, state[0]), "seq", core_swap), origin ^ 1))
    others += near[1:]

    origins = jnp.stack([origin for _, origin in others]).astype(jnp.int32)
    other_docs = docs[origins]
    needed = (origins < shard) & (other_docs[:, -1] >= docs_row[0, 0])
    return attend(
        needed.astype(jnp.int32),
        queries,
        docs_row,
        other_docs.reshape(-1, rows, 1),
        (shard - origins).astype(jnp.int32) * rows,
        [entry for entry, _ in others],
        state,
        True,
        kv_heads,
    )


def solution(mesh):
    in_specs = (
        P("seq", None),
        P(("seq", "vis"), None),
        P(("seq", "vis")),
        P(("seq", "vis")),
        P(),
        P(),
        P(None, "vis"),
        P("vis"),
        P(None, "vis"),
        P(None, "vis"),
        P("vis"),
    )
    return jax.shard_map(
        on_device, mesh=mesh, in_specs=in_specs, out_specs=P("seq", "vis"), check_vma=False
    )
```

profile of v0, /device:TPU:3, one launch (start us, length us, event | category | flops | bytes accessed | tf_op | source)
XLA Modules:
  0.0 134.9 jit_solution(4181574473151500232)
XLA Ops:
  0.7 1.2 copy-done.3
  3.4 1.4 %frame_slots.1 = bf16[64,8320]{1,0:T(8,128)(2,1)S(1)} custom-call(s32[2]{0:T(128)S(1)} %pad_add_fusion.scalars, bf16[64,8192]{1,0:T(8,128)(2,1)S(1)} %copy-done.3, f32[1,8192]{1,0:T(1,128)S(1)} %bitcast.25, s32[1,64]{1,0:T(1,128)S(1)} %bitcast.32), custom_call_target="tpu_custom_call" | custom-call | flops 67108864 | bytes 2097152 | tf_op jit(solution)/shard_map/frame_slots/pallas_call | solution.py:60
  5.6 1.7 %collective-permute-start.2 = (bf16[8,8320]{1,0:T(8,128)(2,1)S(1)}, bf16[8,8320]{1,0:T(8,128)(2,1)S(1)}, u32[]{:S(2)}, u32[]{:S(2)}) collective-permute-start(bf16[8,8320]{1,0:T(8,128)(2,1)S(1)} %get-tuple-element.49), channel_id=1, source_target_pairs={{0,12},{4,8},{8,4},{12,0},{16,28},{20,24},{24,20},{28,16},{1,13},{... | collective-permute-start | bytes 399368 | tf_op jit(solution)/shard_map/ppermute | solution.py:128
  7.3 1.2 collective-permute-start.3
  9.1 1.2 collective-permute-start.5
  10.7 2.4 %collective-permute-start.6 = (bf16[8,8320]{1,0:T(8,128)(2,1)S(1)}, bf16[8,8320]{1,0:T(8,128)(2,1)S(1)}, u32[]{:S(2)}, u32[]{:S(2)}) collective-permute-start(bf16[8,8320]{1,0:T(8,128)(2,1)S(1)} %get-tuple-element.45), channel_id=1, source_target_pairs={{0,28},{4,24},{8,20},{12,16},{16,12},{20,8},{24,4},{28,0},{1,29},{... | collective-permute-start | bytes 399368 | tf_op jit(solution)/shard_map/ppermute | solution.py:128
  13.1 1.4 %collective-permute-done.2.refs_3_ = bf16[8,8320]{1,0:T(8,128)(2,1)S(1)} collective-permute-done((bf16[8,8320]{1,0:T(8,128)(2,1)S(1)}, bf16[8,8320]{1,0:T(8,128)(2,1)S(1)}, u32[]{:S(2)}, u32[]{:S(2)}) %collective-permute-start.2) | collective-permute-done | bytes 133152 | tf_op jit(solution)/shard_map/ppermute | solution.py:128
  14.5 6.7 %collective-permute-done.4.refs_5_ = bf16[8,8320]{1,0:T(8,128)(2,1)S(1)} collective-permute-done((bf16[8,8320]{1,0:T(8,128)(2,1)S(1)}, bf16[8,8320]{1,0:T(8,128)(2,1)S(1)}, u32[]{:S(2)}, u32[]{:S(2)}) %collective-permute-start.4) | collective-permute-done | bytes 133152 | tf_op jit(solution)/shard_map/ppermute | solution.py:128
  21.2 1.4 %collective-permute-start.7 = (bf16[64,2176]{1,0:T(8,128)(2,1)S(1)}, bf16[64,2176]{1,0:T(8,128)(2,1)S(1)}, u32[]{:S(2)}, u32[]{:S(2)}) collective-permute-start(bf16[64,2176]{1,0:T(8,128)(2,1)S(1)} %get-tuple-element.25.refs_0_.refs_6_), channel_id=1, source_target_pairs={{0,1},{2,3},{1,0},{3,2},{4,5},{6,7},{5,4},{7,6},{8,9},{10,11},{9,8... | collective-permute-start | bytes 835592 | tf_op jit(solution)/shard_map/ppermute | solution.py:380
  23.3 3.9 %collective-permute-start.17 = (bf16[64,2048]{1,0:T(8,128)(2,1)S(1)}, bf16[64,2048]{1,0:T(8,128)(2,1)S(1)}, u32[]{:S(2)}, u32[]{:S(2)}) collective-permute-start(bf16[64,2048]{1,0:T(8,128)(2,1)S(1)} %get-tuple-element.28.refs_6_), channel_id=1, source_target_pairs={{0,1},{2,3},{1,0},{3,2},{4,5},{6,7},{5,4},{7,6},{8,9},{10,11},{9,8... | collective-permute-start | bytes 786440 | tf_op jit(solution)/shard_map/ppermute | solution.py:380
  27.9 1.3 collective-permute-start.12
  30.1 4.9 %collective-permute-done.17.refs_7_ = bf16[64,2048]{1,0:T(8,128)(2,1)S(1)} collective-permute-done((bf16[64,2048]{1,0:T(8,128)(2,1)S(1)}, bf16[64,2048]{1,0:T(8,128)(2,1)S(1)}, u32[]{:S(2)}, u32[]{:S(2)}) %collective-permute-start.17) | collective-permute-done | bytes 262176 | tf_op jit(solution)/shard_map/ppermute | solution.py:380
  35.0 1.4 %collective-permute-start.13 = (bf16[64,2048]{1,0:T(8,128)(2,1)S(1)}, bf16[64,2048]{1,0:T(8,128)(2,1)}, u32[]{:S(2)}, u32[]{:S(2)}) collective-permute-start(bf16[64,2048]{1,0:T(8,128)(2,1)S(1)} %get-tuple-element.26.refs_6_), channel_id=1, source_target_pairs={{1,2},{2,1},{5,6},{6,5},{9,10},{10,9},{13,14},{14,13},{17,18},{18,... | collective-permute-start | bytes 786440 | tf_op jit(solution)/shard_map/ppermute | solution.py:380
  36.4 3.2 %collective-permute-start.22 = (bf16[64,2048]{1,0:T(8,128)(2,1)S(1)}, bf16[64,2048]{1,0:T(8,128)(2,1)S(1)}, u32[]{:S(2)}, u32[]{:S(2)}) collective-permute-start(bf16[64,2048]{1,0:T(8,128)(2,1)S(1)} %get-tuple-element.34.refs_6_), channel_id=1, source_target_pairs={{0,1},{2,3},{1,0},{3,2},{4,5},{6,7},{5,4},{7,6},{8,9},{10,11},{9,8... | collective-permute-start | bytes 786440 | tf_op jit(solution)/shard_map/ppermute | solution.py:380
  39.6 1.0 collective-permute-done.12.refs_7_
  40.6 1.4 %collective-permute-start.20 = (bf16[64,2048]{1,0:T(8,128)(2,1)S(1)}, bf16[64,2048]{1,0:T(8,128)(2,1)}, u32[]{:S(2)}, u32[]{:S(2)}) collective-permute-start(bf16[64,2048]{1,0:T(8,128)(2,1)S(1)} %collective-permute-done.17.refs_7_), channel_id=1, source_target_pairs={{1,2},{2,1},{5,6},{6,5},{9,10},{10,9},{13,14},{14,13},{17,18},{18,... | collective-permute-start | bytes 786440 | tf_op jit(solution)/shard_map/ppermute | solution.py:380
  42.0 1.3 collective-permute-start.9
  43.3 1.3 collective-permute-start.11
  45.2 0.8 copy.12.refs_3_
  46.7 2.2 %copy-done = bf16[256,8192]{1,0:T(8,128)(2,1)S(1)} copy-done((bf16[256,8192]{1,0:T(8,128)(2,1)S(1)}, bf16[256,8192]{1,0:T(8,128)(2,1)}, u32[]{:S(2)}) %copy-start) | copy-done | bytes 4194328
  48.8 1.2 text_scale.1.refs_13_
  50.1 0.8 collective-permute-start.23
  50.9 1.3 collective-permute-start.19
  53.6 4.1 %collective-permute-done.11.refs_5_.refs_11_ = bf16[64,2176]{1,0:T(8,128)(2,1)S(1)} collective-permute-done((bf16[64,2176]{1,0:T(8,128)(2,1)S(1)}, bf16[64,2176]{1,0:T(8,128)(2,1)S(1)}, u32[]{:S(2)}, u32[]{:S(2)}) %collective-permute-start.11) | collective-permute-done | bytes 278560 | tf_op jit(solution)/shard_map/ppermute | solution.py:380
  57.7 1.3 collective-permute-start.21
  59.0 3.5 %merge_rows.4 = (bf16[256,2048]{1,0:T(8,128)(2,1)S(1)}, f32[256,512]{1,0:T(8,128)S(1)}) custom-call(bf16[64,2176]{1,0:T(8,128)(2,1)S(1)} %get-tuple-element.25.refs_0_.refs_6_, bf16[64,2176]{1,0:T(8,128)(2,1)S(1)} %collective-permute-done.7.refs_1_.refs_7_, bf16[64,2176]{1,0:T(8,128)(2,1)S(1)} %collective-permute-done.8.refs_2_.refs_8_, ...), custom_call_target="tpu_custom_call" | custom-call | flops 939524096 | bytes 5767168 | tf_op jit(solution)/shard_map/merge_rows/pallas_call | solution.py:192
  62.5 5.6 %queries.3.refs_2_ = f32[256,2048]{1,0:T(8,128)S(1)} custom-call(bf16[256,2048]{1,0:T(8,128)(2,1)S(1)} %get-tuple-element.32.refs_0_, bf16[8192,2048]{1,0:T(8,128)(2,1)} %refs_2_.1, f32[1,2048]{1,0:T(1,128)S(1)} %bitcast.30), custom_call_target="tpu_custom_call" | custom-call | flops 2147483648 | bytes 9437184 | tf_op jit(solution)/shard_map/queries/pallas_call | solution.py:253
  68.1 1.3 collective-permute-start.14
  69.5 1.3 collective-permute-start.24
  70.8 1.3 collective-permute-start.16
  72.1 1.3 collective-permute-start.26
  73.4 3.4 %merge_rows.5 = (bf16[256,2048]{1,0:T(8,128)(2,1)S(1)}, f32[256,512]{1,0:T(8,128)S(1)}) custom-call(bf16[64,2176]{1,0:T(8,128)(2,1)S(1)} %get-tuple-element.25.refs_0_.refs_6_, bf16[64,2176]{1,0:T(8,128)(2,1)S(1)} %collective-permute-done.7.refs_1_.refs_7_, bf16[64,2176]{1,0:T(8,128)(2,1)S(1)} %collective-permute-done.8.refs_2_.refs_8_, ...), custom_call_target="tpu_custom_call" | custom-call | flops 939524096 | bytes 5767168 | tf_op jit(solution)/shard_map/merge_rows/pallas_call | solution.py:192
  76.8 5.6 %queries.4.refs_18_.refs_3_ = f32[256,2048]{1,0:T(8,128)S(1)} custom-call(bf16[256,2048]{1,0:T(8,128)(2,1)S(1)} %get-tuple-element.31.refs_0_, bf16[8192,2048]{1,0:T(8,128)(2,1)} %refs_2_.1, f32[256,2048]{1,0:T(8,128)S(1)} %queries.3.refs_2_), custom_call_target="tpu_custom_call" | custom-call | flops 2147483648 | bytes 9437184 | tf_op jit(solution)/shard_map/queries/pallas_call | solution.py:253
  82.4 1.3 copy-done.1
  83.8 6.8 %collective-permute-done.16.refs_11_ = bf16[64,2048]{1,0:T(8,128)(2,1)S(1)} collective-permute-done((bf16[64,2048]{1,0:T(8,128)(2,1)S(1)}, bf16[64,2048]{1,0:T(8,128)(2,1)S(1)}, u32[]{:S(2)}, u32[]{:S(2)}) %collective-permute-start.16) | collective-permute-done | bytes 262176 | tf_op jit(solution)/shard_map/ppermute | solution.py:380
  90.5 3.3 %merge_rows.6 = (bf16[256,2048]{1,0:T(8,128)(2,1)S(1)}, f32[256,512]{1,0:T(8,128)S(1)}) custom-call(bf16[64,2176]{1,0:T(8,128)(2,1)S(1)} %get-tuple-element.25.refs_0_.refs_6_, bf16[64,2176]{1,0:T(8,128)(2,1)S(1)} %collective-permute-done.7.refs_1_.refs_7_, bf16[64,2176]{1,0:T(8,128)(2,1)S(1)} %collective-permute-done.8.refs_2_.refs_8_, ...), custom_call_target="tpu_custom_call" | custom-call | flops 939524096 | bytes 5767168 | tf_op jit(solution)/shard_map/merge_rows/pallas_call | solution.py:192
  93.9 2.3 %collective-permute-done.26.refs_11_ = bf16[64,2048]{1,0:T(8,128)(2,1)S(1)} collective-permute-done((bf16[64,2048]{1,0:T(8,128)(2,1)S(1)}, bf16[64,2048]{1,0:T(8,128)(2,1)S(1)}, u32[]{:S(2)}, u32[]{:S(2)}) %collective-permute-start.26) | collective-permute-done | bytes 262176 | tf_op jit(solution)/shard_map/ppermute | solution.py:380
  96.2 3.4 %merge_rows.7 = (bf16[256,2048]{1,0:T(8,128)(2,1)S(1)}, bf16[256,512]{1,0:T(8,128)(2,1)S(1)}) custom-call(bf16[64,2176]{1,0:T(8,128)(2,1)S(1)} %get-tuple-element.25.refs_0_.refs_6_, bf16[64,2176]{1,0:T(8,128)(2,1)S(1)} %collective-permute-done.7.refs_1_.refs_7_, bf16[64,2176]{1,0:T(8,128)(2,1)S(1)} %collective-permute-done.8.refs_2_.refs_8_, ...), custom_call_target="tpu_custom_call" | custom-call | flops 939524096 | bytes 5767168 | tf_op jit(solution)/shard_map/merge_rows/pallas_call | solution.py:192
  99.6 3.1 %collective-permute-start.32 = (bf16[256,512]{1,0:T(8,128)(2,1)S(1)}, bf16[256,512]{1,0:T(8,128)(2,1)S(1)}, u32[]{:S(2)}, u32[]{:S(2)}) collective-permute-start(bf16[256,512]{1,0:T(8,128)(2,1)S(1)} %get-tuple-element.39.refs_5_), channel_id=1, source_target_pairs={{8,16},{12,20},{9,17},{13,21},{10,18},{14,22},{11,19},{15,23}} | collective-permute-start | bytes 786440 | tf_op jit(solution)/shard_map/ppermute | solution.py:423
  102.7 1.3 collective-permute-start.30
  104.1 1.3 collective-permute-start.28
  105.4 8.9 %queries.5.refs_1_ = bf16[2,128,2048]{2,1,0:T(8,128)(2,1)S(1)} custom-call(bf16[256,2048]{1,0:T(8,128)(2,1)S(1)} %get-tuple-element.33.refs_0_, bf16[256,2048]{1,0:T(8,128)(2,1)S(1)} %get-tuple-element.36.refs_1_, bf16[8192,2048]{1,0:T(8,128)(2,1)} %refs_2_.1, f32[256,2048]{1,0:T(8,128)S(1)} %copy-done.2), custom_call_target="tpu_custom_call" | custom-call | flops 4294967296 | bytes 18874368 | tf_op jit(solution)/shard_map/queries/pallas_call | solution.py:253
  114.3 2.3 %attend_own.1 = (f32[2,1,2048]{2,1,0:T(1,128)S(1)}, f32[2,1,2048]{2,1,0:T(1,128)S(1)}, f32[2,128,2048]{2,1,0:T(8,128)S(1)}) custom-call(s32[1]{0:T(128)} %constant.9.clone.1.refs_0_, bf16[2,128,2048]{2,1,0:T(8,128)(2,1)S(1)} %queries.5.refs_1_, s32[1,256]{1,0:T(1,128)S(1)} %constant_dynamic-slice_fusion.1.refs_2_, s32[1,256,1]{2,1,0:T(8,128)S(1)} %copy-done.6, ...), custom_call_target="tpu_custom_call" | custom-call | flops 536870912 | bytes 2097152 | tf_op jit(solution)/shard_map/attend_own/pallas_call | solution.py:337
  116.7 1.3 copy-done.10
  118.0 4.1 %collective-permute-start.27 = (bf16[256,512]{1,0:T(8,128)(2,1)S(1)}, bf16[256,512]{1,0:T(8,128)(2,1)S(1)}, u32[]{:S(2)}, u32[]{:S(2)}) collective-permute-start(bf16[256,512]{1,0:T(8,128)(2,1)S(1)} %get-tuple-element.39.refs_5_), channel_id=1, source_target_pairs={{0,4},{4,0},{8,12},{12,8},{16,20},{20,16},{24,28},{28,24},{1,5},{5... | collective-permute-start | bytes 786440 | tf_op jit(solution)/shard_map/ppermute | solution.py:433
  122.7 0.9 fusion
  124.6 1.6 %copy-done.11 = f32[2,128,2048]{2,1,0:T(8,128)S(1)} copy-done((f32[2,128,2048]{2,1,0:T(8,128)S(1)}, f32[2,128,2048]{2,1,0:T(8,128)}, u32[]{:S(2)}) %copy-start.11) | copy-done | bytes 2097176
  126.2 8.7 %attend_rest.1 = bf16[256,2048]{1,0:T(8,128)(2,1)} custom-call(s32[7]{0:T(128)S(1)} %and_convert_fusion.refs_0_, bf16[2,128,2048]{2,1,0:T(8,128)(2,1)S(1)} %queries.5.refs_1_, s32[1,256]{1,0:T(1,128)S(1)} %constant_dynamic-slice_fusion.1.refs_2_, s32[7,256,1]{2,1,0:T(8,128)S(1)} %copy.13.refs_3_, s32[7]{0:T(128)S(1)} %subtract_multiply_fusion.refs_4_, ...), custom_call_target="tpu_custom_call" | custom-call | flops 3758096384 | bytes 2097152 | tf_op jit(solution)/shard_map/attend_rest/pallas_call | solution.py:337
  (74 shorter events, 9.8 us)
Async XLA Ops:
  0.7 1.2 copy-start.3
  2.0 0.8 copy-start.4
  2.7 0.7 copy-start.9
  4.7 25.3 %copy-start.12 = (s32[2048]{0:T(1024)S(1)}, s32[2048]{0:T(1024)}, u32[]{:S(2)}) copy-start(s32[2048]{0:T(1024)} %param.15) | copy-start | bytes 24580
  4.8 4.2 %collective-permute-start = (bf16[8,8320]{1,0:T(8,128)(2,1)S(1)}, bf16[8,8320]{1,0:T(8,128)(2,1)S(1)}, u32[]{:S(2)}, u32[]{:S(2)}) collective-permute-start(bf16[8,8320]{1,0:T(8,128)(2,1)S(1)} %get-tuple-element.51), channel_id=1, source_target_pairs={{0,4},{4,0},{8,12},{12,8},{16,20},{20,16},{24,28},{28,24},{1,5},{5... | collective-permute-start | bytes 399368 | tf_op jit(solution)/shard_map/ppermute | solution.py:128
  5.6 5.1 %collective-permute-start.1 = (bf16[8,8320]{1,0:T(8,128)(2,1)S(1)}, bf16[8,8320]{1,0:T(8,128)(2,1)S(1)}, u32[]{:S(2)}, u32[]{:S(2)}) collective-permute-start(bf16[8,8320]{1,0:T(8,128)(2,1)S(1)} %get-tuple-element.50), channel_id=1, source_target_pairs={{0,8},{4,12},{8,0},{12,4},{16,24},{20,28},{24,16},{28,20},{1,9},{5... | collective-permute-start | bytes 399368 | tf_op jit(solution)/shard_map/ppermute | solution.py:128
  5.6 8.9 %collective-permute-start.2 = (bf16[8,8320]{1,0:T(8,128)(2,1)S(1)}, bf16[8,8320]{1,0:T(8,128)(2,1)S(1)}, u32[]{:S(2)}, u32[]{:S(2)}) collective-permute-start(bf16[8,8320]{1,0:T(8,128)(2,1)S(1)} %get-tuple-element.49), channel_id=1, source_target_pairs={{0,12},{4,8},{8,4},{12,0},{16,28},{20,24},{24,20},{28,16},{1,13},{... | collective-permute-start | bytes 399368 | tf_op jit(solution)/shard_map/ppermute | solution.py:128
  7.3 7.2 %collective-permute-start.3 = (bf16[8,8320]{1,0:T(8,128)(2,1)S(1)}, bf16[8,8320]{1,0:T(8,128)(2,1)S(1)}, u32[]{:S(2)}, u32[]{:S(2)}) collective-permute-start(bf16[8,8320]{1,0:T(8,128)(2,1)S(1)} %get-tuple-element.48), channel_id=1, source_target_pairs={{0,16},{4,20},{8,24},{12,28},{16,0},{20,4},{24,8},{28,12},{1,17},{... | collective-permute-start | bytes 399368 | tf_op jit(solution)/shard_map/ppermute | solution.py:128
  8.5 12.6 %collective-permute-start.4 = (bf16[8,8320]{1,0:T(8,128)(2,1)S(1)}, bf16[8,8320]{1,0:T(8,128)(2,1)S(1)}, u32[]{:S(2)}, u32[]{:S(2)}) collective-permute-start(bf16[8,8320]{1,0:T(8,128)(2,1)S(1)} %get-tuple-element.47), channel_id=1, source_target_pairs={{0,20},{4,16},{8,28},{12,24},{16,4},{20,0},{24,12},{28,8},{1,21},{... | collective-permute-start | bytes 399368 | tf_op jit(solution)/shard_map/ppermute | solution.py:128
  9.1 12.0 %collective-permute-start.5 = (bf16[8,8320]{1,0:T(8,128)(2,1)S(1)}, bf16[8,8320]{1,0:T(8,128)(2,1)S(1)}, u32[]{:S(2)}, u32[]{:S(2)}) collective-permute-start(bf16[8,8320]{1,0:T(8,128)(2,1)S(1)} %get-tuple-element.46), channel_id=1, source_target_pairs={{0,24},{4,28},{8,16},{12,20},{16,8},{20,12},{24,0},{28,4},{1,25},{... | collective-permute-start | bytes 399368 | tf_op jit(solution)/shard_map/ppermute | solution.py:128
  10.7 10.4 %collective-permute-start.6 = (bf16[8,8320]{1,0:T(8,128)(2,1)S(1)}, bf16[8,8320]{1,0:T(8,128)(2,1)S(1)}, u32[]{:S(2)}, u32[]{:S(2)}) collective-permute-start(bf16[8,8320]{1,0:T(8,128)(2,1)S(1)} %get-tuple-element.45), channel_id=1, source_target_pairs={{0,28},{4,24},{8,20},{12,16},{16,12},{20,8},{24,4},{28,0},{1,29},{... | collective-permute-start | bytes 399368 | tf_op jit(solution)/shard_map/ppermute | solution.py:128
  21.2 8.2 %collective-permute-start.7 = (bf16[64,2176]{1,0:T(8,128)(2,1)S(1)}, bf16[64,2176]{1,0:T(8,128)(2,1)S(1)}, u32[]{:S(2)}, u32[]{:S(2)}) collective-permute-start(bf16[64,2176]{1,0:T(8,128)(2,1)S(1)} %get-tuple-element.25.refs_0_.refs_6_), channel_id=1, source_target_pairs={{0,1},{2,3},{1,0},{3,2},{4,5},{6,7},{5,4},{7,6},{8,9},{10,11},{9,8... | collective-permute-start | bytes 835592 | tf_op jit(solution)/shard_map/ppermute | solution.py:380
  22.7 19.3 %collective-permute-start.8 = (bf16[64,2176]{1,0:T(8,128)(2,1)S(1)}, bf16[64,2176]{1,0:T(8,128)(2,1)S(1)}, u32[]{:S(2)}, u32[]{:S(2)}) collective-permute-start(bf16[64,2176]{1,0:T(8,128)(2,1)S(1)} %get-tuple-element.25.refs_0_.refs_6_), channel_id=1, source_target_pairs={{1,2},{2,1},{5,6},{6,5},{9,10},{10,9},{13,14},{14,13},{17,18},{18,... | collective-permute-start | bytes 835592 | tf_op jit(solution)/shard_map/ppermute | solution.py:380
  23.3 11.7 %collective-permute-start.17 = (bf16[64,2048]{1,0:T(8,128)(2,1)S(1)}, bf16[64,2048]{1,0:T(8,128)(2,1)S(1)}, u32[]{:S(2)}, u32[]{:S(2)}) collective-permute-start(bf16[64,2048]{1,0:T(8,128)(2,1)S(1)} %get-tuple-element.28.refs_6_), channel_id=1, source_target_pairs={{0,1},{2,3},{1,0},{3,2},{4,5},{6,7},{5,4},{7,6},{8,9},{10,11},{9,8... | collective-permute-start | bytes 786440 | tf_op jit(solution)/shard_map/ppermute | solution.py:380
  27.2 9.2 %collective-permute-start.18 = (bf16[64,2048]{1,0:T(8,128)(2,1)S(1)}, bf16[64,2048]{1,0:T(8,128)(2,1)S(1)}, u32[]{:S(2)}, u32[]{:S(2)}) collective-permute-start(bf16[64,2048]{1,0:T(8,128)(2,1)S(1)} %get-tuple-element.28.refs_6_), channel_id=1, source_target_pairs={{1,2},{2,1},{5,6},{6,5},{9,10},{10,9},{13,14},{14,13},{17,18},{18,... | collective-permute-start | bytes 786440 | tf_op jit(solution)/shard_map/ppermute | solution.py:380
  27.9 12.7 %collective-permute-start.12 = (bf16[64,2048]{1,0:T(8,128)(2,1)S(1)}, bf16[64,2048]{1,0:T(8,128)(2,1)S(1)}, u32[]{:S(2)}, u32[]{:S(2)}) collective-permute-start(bf16[64,2048]{1,0:T(8,128)(2,1)S(1)} %get-tuple-element.26.refs_6_), channel_id=1, source_target_pairs={{0,1},{2,3},{1,0},{3,2},{4,5},{6,7},{5,4},{7,6},{8,9},{10,11},{9,8... | collective-permute-start | bytes 786440 | tf_op jit(solution)/shard_map/ppermute | solution.py:380
  29.4 13.9 %collective-permute-start.10 = (bf16[64,2176]{1,0:T(8,128)(2,1)S(1)}, bf16[64,2176]{1,0:T(8,128)(2,1)S(1)}, u32[]{:S(2)}, u32[]{:S(2)}) collective-permute-start(bf16[64,2176]{1,0:T(8,128)(2,1)S(1)} %collective-permute-done.7.refs_1_.refs_7_), channel_id=1, source_target_pairs={{1,2},{2,1},{5,6},{6,5},{9,10},{10,9},{13,14},{14,13},{17,18},{18,... | collective-permute-start | bytes 835592 | tf_op jit(solution)/shard_map/ppermute | solution.py:380
  35.0 15.1 %collective-permute-start.13 = (bf16[64,2048]{1,0:T(8,128)(2,1)S(1)}, bf16[64,2048]{1,0:T(8,128)(2,1)}, u32[]{:S(2)}, u32[]{:S(2)}) collective-permute-start(bf16[64,2048]{1,0:T(8,128)(2,1)S(1)} %get-tuple-element.26.refs_6_), channel_id=1, source_target_pairs={{1,2},{2,1},{5,6},{6,5},{9,10},{10,9},{13,14},{14,13},{17,18},{18,... | collective-permute-start | bytes 786440 | tf_op jit(solution)/shard_map/ppermute | solution.py:380
  36.4 14.5 %collective-permute-start.22 = (bf16[64,2048]{1,0:T(8,128)(2,1)S(1)}, bf16[64,2048]{1,0:T(8,128)(2,1)S(1)}, u32[]{:S(2)}, u32[]{:S(2)}) collective-permute-start(bf16[64,2048]{1,0:T(8,128)(2,1)S(1)} %get-tuple-element.34.refs_6_), channel_id=1, source_target_pairs={{0,1},{2,3},{1,0},{3,2},{4,5},{6,7},{5,4},{7,6},{8,9},{10,11},{9,8... | collective-permute-start | bytes 786440 | tf_op jit(solution)/shard_map/ppermute | solution.py:380
  40.6 11.6 %collective-permute-start.20 = (bf16[64,2048]{1,0:T(8,128)(2,1)S(1)}, bf16[64,2048]{1,0:T(8,128)(2,1)}, u32[]{:S(2)}, u32[]{:S(2)}) collective-permute-start(bf16[64,2048]{1,0:T(8,128)(2,1)S(1)} %collective-permute-done.17.refs_7_), channel_id=1, source_target_pairs={{1,2},{2,1},{5,6},{6,5},{9,10},{10,9},{13,14},{14,13},{17,18},{18,... | collective-permute-start | bytes 786440 | tf_op jit(solution)/shard_map/ppermute | solution.py:380
  42.0 11.0 %collective-permute-start.9 = (bf16[64,2176]{1,0:T(8,128)(2,1)S(1)}, bf16[64,2176]{1,0:T(8,128)(2,1)S(1)}, u32[]{:S(2)}, u32[]{:S(2)}) collective-permute-start(bf16[64,2176]{1,0:T(8,128)(2,1)S(1)} %collective-permute-done.8.refs_2_.refs_8_), channel_id=1, source_target_pairs={{2,3},{1,0},{6,7},{5,4},{10,11},{9,8},{14,15},{13,12},{18,19},{17,... | collective-permute-start | bytes 835592 | tf_op jit(solution)/shard_map/ppermute | solution.py:380
  43.3 14.4 %collective-permute-start.11 = (bf16[64,2176]{1,0:T(8,128)(2,1)S(1)}, bf16[64,2176]{1,0:T(8,128)(2,1)S(1)}, u32[]{:S(2)}, u32[]{:S(2)}) collective-permute-start(bf16[64,2176]{1,0:T(8,128)(2,1)S(1)} %collective-permute-done.10.refs_4_.refs_10_), channel_id=1, source_target_pairs={{2,3},{1,0},{6,7},{5,4},{10,11},{9,8},{14,15},{13,12},{18,19},{17,... | collective-permute-start | bytes 835592 | tf_op jit(solution)/shard_map/ppermute | solution.py:380
  46.6 2.2 %copy-start = (bf16[256,8192]{1,0:T(8,128)(2,1)S(1)}, bf16[256,8192]{1,0:T(8,128)(2,1)}, u32[]{:S(2)}) copy-start(bf16[256,8192]{1,0:T(8,128)(2,1)} %refs_12_.7) | copy-start | bytes 12582916
  48.8 10.1 %copy-start.5 = (f32[8192]{0:T(1024)S(1)}, f32[8192]{0:T(1024)}, u32[]{:S(2)}) copy-start(f32[8192]{0:T(1024)} %param.16) | copy-start | bytes 98308
  50.1 12.4 %copy-start.7 = (f32[2048]{0:T(1024)S(1)}, f32[2048]{0:T(1024)}, u32[]{:S(2)}) copy-start(f32[2048]{0:T(1024)} %param.18) | copy-start | bytes 24580
  50.1 18.0 %collective-permute-start.23 = (bf16[64,2048]{1,0:T(8,128)(2,1)S(1)}, bf16[64,2048]{1,0:T(8,128)(2,1)S(1)}, u32[]{:S(2)}, u32[]{:S(2)}) collective-permute-start(bf16[64,2048]{1,0:T(8,128)(2,1)S(1)} %get-tuple-element.34.refs_6_), channel_id=1, source_target_pairs={{1,2},{2,1},{5,6},{6,5},{9,10},{10,9},{13,14},{14,13},{17,18},{18,... | collective-permute-start | bytes 786440 | tf_op jit(solution)/shard_map/ppermute | solution.py:380
  50.9 18.5 %collective-permute-start.19 = (bf16[64,2048]{1,0:T(8,128)(2,1)S(1)}, bf16[64,2048]{1,0:T(8,128)(2,1)S(1)}, u32[]{:S(2)}, u32[]{:S(2)}) collective-permute-start(bf16[64,2048]{1,0:T(8,128)(2,1)S(1)} %collective-permute-done.18.refs_8_), channel_id=1, source_target_pairs={{2,3},{1,0},{6,7},{5,4},{10,11},{9,8},{14,15},{13,12},{18,19},{17,... | collective-permute-start | bytes 786440 | tf_op jit(solution)/shard_map/ppermute | solution.py:380
  52.2 18.5 %collective-permute-start.15 = (bf16[64,2048]{1,0:T(8,128)(2,1)S(1)}, bf16[64,2048]{1,0:T(8,128)(2,1)S(1)}, u32[]{:S(2)}, u32[]{:S(2)}) collective-permute-start(bf16[64,2048]{1,0:T(8,128)(2,1)S(1)} %collective-permute-done.12.refs_7_), channel_id=1, source_target_pairs={{1,2},{2,1},{5,6},{6,5},{9,10},{10,9},{13,14},{14,13},{17,18},{18,... | collective-permute-start | bytes 786440 | tf_op jit(solution)/shard_map/ppermute | solution.py:380
  52.9 19.1 %collective-permute-start.25 = (bf16[64,2048]{1,0:T(8,128)(2,1)S(1)}, bf16[64,2048]{1,0:T(8,128)(2,1)S(1)}, u32[]{:S(2)}, u32[]{:S(2)}) collective-permute-start(bf16[64,2048]{1,0:T(8,128)(2,1)S(1)} %collective-permute-done.22.refs_7_), channel_id=1, source_target_pairs={{1,2},{2,1},{5,6},{6,5},{9,10},{10,9},{13,14},{14,13},{17,18},{18,... | collective-permute-start | bytes 786440 | tf_op jit(solution)/shard_map/ppermute | solution.py:380
  57.7 15.7 %collective-permute-start.21 = (bf16[64,2048]{1,0:T(8,128)(2,1)}, bf16[64,2048]{1,0:T(8,128)(2,1)S(1)}, u32[]{:S(2)}, u32[]{:S(2)}) collective-permute-start(bf16[64,2048]{1,0:T(8,128)(2,1)} %collective-permute-done.20.refs_10_), channel_id=1, source_target_pairs={{2,3},{1,0},{6,7},{5,4},{10,11},{9,8},{14,15},{13,12},{18,19},{17,... | collective-permute-start | bytes 786440 | tf_op jit(solution)/shard_map/ppermute | solution.py:380
  68.1 15.6 %collective-permute-start.14 = (bf16[64,2048]{1,0:T(8,128)(2,1)}, bf16[64,2048]{1,0:T(8,128)(2,1)S(1)}, u32[]{:S(2)}, u32[]{:S(2)}) collective-permute-start(bf16[64,2048]{1,0:T(8,128)(2,1)} %collective-permute-done.13.refs_8_), channel_id=1, source_target_pairs={{2,3},{1,0},{6,7},{5,4},{10,11},{9,8},{14,15},{13,12},{18,19},{17,... | collective-permute-start | bytes 786440 | tf_op jit(solution)/shard_map/ppermute | solution.py:380
  69.5 24.4 %collective-permute-start.24 = (bf16[64,2048]{1,0:T(8,128)(2,1)S(1)}, bf16[64,2048]{1,0:T(8,128)(2,1)S(1)}, u32[]{:S(2)}, u32[]{:S(2)}) collective-permute-start(bf16[64,2048]{1,0:T(8,128)(2,1)S(1)} %collective-permute-done.23.refs_8_), channel_id=1, source_target_pairs={{2,3},{1,0},{6,7},{5,4},{10,11},{9,8},{14,15},{13,12},{18,19},{17,... | collective-permute-start | bytes 786440 | tf_op jit(solution)/shard_map/ppermute | solution.py:380
  70.8 19.8 %collective-permute-start.16 = (bf16[64,2048]{1,0:T(8,128)(2,1)S(1)}, bf16[64,2048]{1,0:T(8,128)(2,1)S(1)}, u32[]{:S(2)}, u32[]{:S(2)}) collective-permute-start(bf16[64,2048]{1,0:T(8,128)(2,1)S(1)} %collective-permute-done.15.refs_10_), channel_id=1, source_target_pairs={{2,3},{1,0},{6,7},{5,4},{10,11},{9,8},{14,15},{13,12},{18,19},{17,... | collective-permute-start | bytes 786440 | tf_op jit(solution)/shard_map/ppermute | solution.py:380
  72.1 24.1 %collective-permute-start.26 = (bf16[64,2048]{1,0:T(8,128)(2,1)S(1)}, bf16[64,2048]{1,0:T(8,128)(2,1)S(1)}, u32[]{:S(2)}, u32[]{:S(2)}) collective-permute-start(bf16[64,2048]{1,0:T(8,128)(2,1)S(1)} %collective-permute-done.25.refs_10_), channel_id=1, source_target_pairs={{2,3},{1,0},{6,7},{5,4},{10,11},{9,8},{14,15},{13,12},{18,19},{17,... | collective-permute-start | bytes 786440 | tf_op jit(solution)/shard_map/ppermute | solution.py:380
  82.4 1.3 copy-start.1
  90.5 5.6 %copy-start.8 = (f32[256]{0:T(256)S(1)}, f32[256]{0:T(256)}, u32[]{:S(2)}) copy-start(f32[256]{0:T(256)} %param.21) | copy-start | bytes 3076
  96.2 9.2 %copy-start.2 = (f32[256,2048]{1,0:T(8,128)S(1)}, f32[256,2048]{1,0:T(8,128)}, u32[]{:S(2)}) copy-start(f32[256,2048]{1,0:T(8,128)} %copy-done.1) | copy-start | bytes 6291460
  99.6 22.5 %collective-permute-start.32 = (bf16[256,512]{1,0:T(8,128)(2,1)S(1)}, bf16[256,512]{1,0:T(8,128)(2,1)S(1)}, u32[]{:S(2)}, u32[]{:S(2)}) collective-permute-start(bf16[256,512]{1,0:T(8,128)(2,1)S(1)} %get-tuple-element.39.refs_5_), channel_id=1, source_target_pairs={{8,16},{12,20},{9,17},{13,21},{10,18},{14,22},{11,19},{15,23}} | collective-permute-start | bytes 786440 | tf_op jit(solution)/shard_map/ppermute | solution.py:423
  102.7 19.4 %collective-permute-start.30 = (bf16[256,512]{1,0:T(8,128)(2,1)S(1)}, bf16[256,512]{1,0:T(8,128)(2,1)S(1)}, u32[]{:S(2)}, u32[]{:S(2)}) collective-permute-start(bf16[256,512]{1,0:T(8,128)(2,1)S(1)} %get-tuple-element.39.refs_5_), channel_id=1, source_target_pairs={{0,16},{4,20},{8,24},{12,28},{1,17},{5,21},{9,25},{13,29},{2,18},{... | collective-permute-start | bytes 786440 | tf_op jit(solution)/shard_map/ppermute | solution.py:423
  104.1 18.6 %collective-permute-start.28 = (bf16[256,512]{1,0:T(8,128)(2,1)S(1)}, bf16[256,512]{1,0:T(8,128)(2,1)S(1)}, u32[]{:S(2)}, u32[]{:S(2)}) collective-permute-start(bf16[256,512]{1,0:T(8,128)(2,1)S(1)} %get-tuple-element.39.refs_5_), channel_id=1, source_target_pairs={{0,8},{4,12},{16,24},{20,28},{1,9},{5,13},{17,25},{21,29},{2,10},{... | collective-permute-start | bytes 786440 | tf_op jit(solution)/shard_map/ppermute | solution.py:423
  105.4 9.0 %copy-start.6 = (s32[1,256,1]{2,1,0:T(8,128)S(1)}, s32[1,256,1]{2,1,0:T(8,128)}, u32[]{:S(2)}) copy-start(s32[1,256,1]{2,1,0:T(8,128)} %copy.12.refs_3_) | copy-start | bytes 3076
  116.7 1.3 copy-start.10
  118.0 5.9 %collective-permute-start.27 = (bf16[256,512]{1,0:T(8,128)(2,1)S(1)}, bf16[256,512]{1,0:T(8,128)(2,1)S(1)}, u32[]{:S(2)}, u32[]{:S(2)}) collective-permute-start(bf16[256,512]{1,0:T(8,128)(2,1)S(1)} %get-tuple-element.39.refs_5_), channel_id=1, source_target_pairs={{0,4},{4,0},{8,12},{12,8},{16,20},{20,16},{24,28},{28,24},{1,5},{5... | collective-permute-start | bytes 786440 | tf_op jit(solution)/shard_map/ppermute | solution.py:433
  122.1 1.8 %collective-permute-start.33 = (bf16[256,512]{1,0:T(8,128)(2,1)S(1)}, bf16[256,512]{1,0:T(8,128)(2,1)}, u32[]{:S(2)}, u32[]{:S(2)}) collective-permute-start(bf16[256,512]{1,0:T(8,128)(2,1)S(1)} %collective-permute-done.32.refs_11_), channel_id=1, source_target_pairs={{0,4},{4,0},{8,12},{12,8},{16,20},{20,16},{24,28},{28,24},{1,5},{5... | collective-permute-start | bytes 786440 | tf_op jit(solution)/shard_map/ppermute | solution.py:433
  122.2 2.0 %collective-permute-start.31 = (bf16[256,512]{1,0:T(8,128)(2,1)S(1)}, bf16[256,512]{1,0:T(8,128)(2,1)}, u32[]{:S(2)}, u32[]{:S(2)}) collective-permute-start(bf16[256,512]{1,0:T(8,128)(2,1)S(1)} %collective-permute-done.30.refs_10_), channel_id=1, source_target_pairs={{0,4},{4,0},{8,12},{12,8},{16,20},{20,16},{24,28},{28,24},{1,5},{5... | collective-permute-start | bytes 786440 | tf_op jit(solution)/shard_map/ppermute | solution.py:433
  122.7 1.9 %collective-permute-start.29 = (bf16[256,512]{1,0:T(8,128)(2,1)S(1)}, bf16[256,512]{1,0:T(8,128)(2,1)}, u32[]{:S(2)}, u32[]{:S(2)}) collective-permute-start(bf16[256,512]{1,0:T(8,128)(2,1)S(1)} %collective-permute-done.28.refs_9_), channel_id=1, source_target_pairs={{0,4},{4,0},{8,12},{12,8},{16,20},{20,16},{24,28},{28,24},{1,5},{5... | collective-permute-start | bytes 786440 | tf_op jit(solution)/shard_map/ppermute | solution.py:433
  124.6 1.6 %copy-start.11 = (f32[2,128,2048]{2,1,0:T(8,128)S(1)}, f32[2,128,2048]{2,1,0:T(8,128)}, u32[]{:S(2)}) copy-start(f32[2,128,2048]{2,1,0:T(8,128)} %copy-done.10) | copy-start | bytes 6291460
where the time goes:
time: 136 us; the launch traced here: 135 us
  Pallas kernels  47.6 us (35%)
  starting transfers between devices  45.3 us (33%)
  waiting for transfers between devices  28.2 us (21%)
  local copies, waits for them, and re-layouts  11.7 us (9%)
    ppermute x20, starting transfers between devices, hop(): found[c][s, odd] = lax.ppermute(sent, 'vis', pairs)  27 us
    pallas_call x3, Pallas kernels, project_queries(): pl.pallas_call(functools.partial(query_kernel, parts=len(parts), finish=g...  20.2 us
    ppermute x20, waiting for transfers between devices, hop(): found[c][s, odd] = lax.ppermute(sent, 'vis', pairs)  19.2 us
    pallas_call x4, Pallas kernels, merge_chunk(): pl.pallas_call(functools.partial(merge_kernel, blocks=blocks, rows=rows,...  13.7 us
    pallas_call x2, Pallas kernels, attend(): pl.pallas_call(functools.partial(attend_kernel, blocks=blocks, kv_heads=k...  11 us
    unnamed x26, local copies, waits for them, and re-layouts  9.11 us
    ppermute x7, waiting for transfers between devices, swap_slots(): parts.append(lax.ppermute(sent, 'seq', [(i, i ^ d) for i in range(count)]))  8.39 us
    ppermute x7, starting transfers between devices, swap_slots(): parts.append(lax.ppermute(sent, 'seq', [(i, i ^ d) for i in range(count)]))  7.88 us
  transfers between devices with their start and end apart: 34, of which 11 were waited for; matrix products, arithmetic and copies ran while one was open for 3% of the time, Pallas kernels for 25%

commit v1 on v0

--- a/solution.py
+++ b/solution.py
@@ -32,7 +32,19 @@
     return (widened * lax.rsqrt(mean_square + EPSILON) * gain).astype(BF16)
 
 
-def slots_kernel(scalars, frames, gain, place_row, out, *, shard_rows, capacity):
+def slots_kernel(
+    scalars, frames_in, gain_in, places_in, out, frames, gain, place_row, sems, *, shard_rows, capacity
+):
+    fetches = [
+        pltpu.make_async_copy(source, target, sems.at[i])
+        for i, (source, target) in enumerate(
+            ((places_in, place_row), (gain_in, gain), (frames_in, frames))
+        )
+    ]
+    for fetch in fetches:
+        fetch.start()
+    for fetch in fetches:
+        fetch.wait()
     count, shard = scalars[0], scalars[1]
     rows, width = frames.shape
     across = lax.broadcasted_iota(jnp.int32, (rows, rows), 1)
@@ -61,8 +73,14 @@
         functools.partial(slots_kernel, shard_rows=shard_rows, capacity=capacity),
         out_shape=jax.ShapeDtypeStruct((rows, width + META), BF16),
         in_specs=[pl.BlockSpec(memory_space=pltpu.SMEM)]
-        + [pl.BlockSpec(memory_space=pltpu.VMEM)] * 3,
+        + [pl.BlockSpec(memory_space=pl.ANY)] * 3,
         out_specs=pl.BlockSpec(memory_space=pltpu.VMEM),
+        scratch_shapes=[
+            pltpu.VMEM((rows, width), BF16),
+            pltpu.VMEM((1, width), F32),
+            pltpu.VMEM((1, rows), jnp.int32),
+            pltpu.SemaphoreType.DMA((3,)),
+        ],
         compiler_params=params(),
         cost_estimate=cost(2 * rows * rows * width, 4 * rows * width),
         name="frame_slots",
@@ -403,14 +421,14 @@
     for s in range(1, vis_count):
         for c in range(CHUNKS):
             hop(c, s)
+    half = CHUNKS // 2
     for c in range(CHUNKS):
-        if c == 2:
-            query(0)
-            query(1)
-        merge(c, *([sums["queries"]] if c == 2 else []))
+        if c == half:
+            for b in range(half):
+                query(b)
+        merge(c, *([sums["queries"]] if c == half else []))
     keyval = sums["total"]
 
-    half = CHUNKS // 2
     queries = project_queries(
         merged[half:], w_query, half * chunk, sums["queries"], kv_heads
     )
@@ -424,18 +442,15 @@
     docs = doc_ids.reshape(seq_count, rows)
     docs_row = lax.dynamic_slice_in_dim(docs, shard, 1)
     docs_own = docs_row.reshape(1, rows, 1)
-    one = jnp.ones((1,), jnp.int32)
-    state = attend(
-        one, queries, docs_row, docs_own, 0 * one, [keyval], None, False, kv_heads
-    )
     core_swap = [(i, i ^ 1) for i in range(seq_count)]
     for held, origin in near:
-        others.append((lax.ppermute(after(held, state[0]), "seq", core_swap), origin ^ 1))
-    others += near[1:]
+        held = after(held, queries)
+        others.append((lax.ppermute(held, "seq", core_swap), origin ^ 1))
+    others += near
 
     origins = jnp.stack([origin for _, origin in others]).astype(jnp.int32)
     other_docs = docs[origins]
-    needed = (origins < shard) & (other_docs[:, -1] >= docs_row[0, 0])
+    needed = (origins <= shard) & (other_docs[:, -1] >= docs_row[0, 0])
     return attend(
         needed.astype(jnp.int32),
         queries,
@@ -443,7 +458,7 @@
         other_docs.reshape(-1, rows, 1),
         (shard - origins).astype(jnp.int32) * rows,
         [entry for entry, _ in others],
-        state,
+        None,
         True,
         kv_heads,
     )

time: 136 us -> 134 us (0.985)
  the two profiles are of different devices: /device:TPU:3 before, /device:TPU:5 now
where the time goes in v1:
time: 134 us
  Pallas kernels  49.6 us (37%)
  starting transfers between devices  44.5 us (33%)
  waiting for transfers between devices  27.6 us (21%)
  local copies, waits for them, and re-layouts  9.02 us (7%)
  other arithmetic  2.19 us (2%)
    ppermute x20, starting transfers between devices, hop(): found[c][s, odd] = lax.ppermute(sent, 'vis', pairs)  26.9 us
    pallas_call x3, Pallas kernels, project_queries(): pl.pallas_call(functools.partial(query_kernel, parts=len(parts), finish=g...  20.1 us
    ppermute x20, waiting for transfers between devices, hop(): found[c][s, odd] = lax.ppermute(sent, 'vis', pairs)  17.7 us
    pallas_call x4, Pallas kernels, merge_chunk(): pl.pallas_call(functools.partial(merge_kernel, blocks=blocks, rows=rows,...  13.7 us
    pallas_call x1, Pallas kernels, attend(): pl.pallas_call(functools.partial(attend_kernel, blocks=blocks, kv_heads=k...  13 us
    ppermute x7, waiting for transfers between devices, swap_slots(): parts.append(lax.ppermute(sent, 'seq', [(i, i ^ d) for i in range(count)]))  8.54 us
    ppermute x7, starting transfers between devices, swap_slots(): parts.append(lax.ppermute(sent, 'seq', [(i, i ^ d) for i in range(count)]))  7.76 us
    unnamed x24, local copies, waits for them, and re-layouts  6.18 us
  transfers between devices with their start and end apart: 34, of which 13 were waited for; matrix products, arithmetic and copies ran while one was open for 4% of the time, Pallas kernels for 24%

profile of v1, /device:TPU:5, one launch (start us, length us, event | category | flops | bytes accessed | tf_op | source)
XLA Modules:
  0.0 134.0 jit_solution(6421274960317033621)
XLA Ops:
  0.7 1.2 copy-done.3
  2.0 0.8 copy-done.4
  3.4 1.5 %frame_slots.1 = bf16[64,8320]{1,0:T(8,128)(2,1)S(1)} custom-call(s32[2]{0:T(128)S(1)} %pad_add_fusion.scalars, bf16[64,8192]{1,0:T(8,128)(2,1)S(1)} %copy-done.3, f32[1,8192]{1,0:T(1,128)S(1)} %bitcast.24, s32[1,64]{1,0:T(1,128)S(1)} %bitcast.31), custom_call_target="tpu_custom_call" | custom-call | flops 67108864 | bytes 2097152 | tf_op jit(solution)/shard_map/frame_slots/pallas_call | solution.py:72
  5.0 0.8 collective-permute-start
  5.7 1.2 collective-permute-start.1
  7.5 1.8 %collective-permute-start.4 = (bf16[8,8320]{1,0:T(8,128)(2,1)S(1)}, bf16[8,8320]{1,0:T(8,128)(2,1)S(1)}, u32[]{:S(2)}, u32[]{:S(2)}) collective-permute-start(bf16[8,8320]{1,0:T(8,128)(2,1)S(1)} %get-tuple-element.41), channel_id=1, source_target_pairs={{0,20},{4,16},{8,28},{12,24},{16,4},{20,0},{24,12},{28,8},{1,21},{... | collective-permute-start | bytes 399368 | tf_op jit(solution)/shard_map/ppermute | solution.py:146
  9.3 1.1 collective-permute-start.5
  10.9 2.3 %collective-permute-start.6 = (bf16[8,8320]{1,0:T(8,128)(2,1)S(1)}, bf16[8,8320]{1,0:T(8,128)(2,1)S(1)}, u32[]{:S(2)}, u32[]{:S(2)}) collective-permute-start(bf16[8,8320]{1,0:T(8,128)(2,1)S(1)} %get-tuple-element.39), channel_id=1, source_target_pairs={{0,28},{4,24},{8,20},{12,16},{16,12},{20,8},{24,4},{28,0},{1,29},{... | collective-permute-start | bytes 399368 | tf_op jit(solution)/shard_map/ppermute | solution.py:146
  13.2 1.4 %collective-permute-done.2.refs_3_ = bf16[8,8320]{1,0:T(8,128)(2,1)S(1)} collective-permute-done((bf16[8,8320]{1,0:T(8,128)(2,1)S(1)}, bf16[8,8320]{1,0:T(8,128)(2,1)S(1)}, u32[]{:S(2)}, u32[]{:S(2)}) %collective-permute-start.2) | collective-permute-done | bytes 133152 | tf_op jit(solution)/shard_map/ppermute | solution.py:146
  14.6 6.7 %collective-permute-done.4.refs_5_ = bf16[8,8320]{1,0:T(8,128)(2,1)S(1)} collective-permute-done((bf16[8,8320]{1,0:T(8,128)(2,1)S(1)}, bf16[8,8320]{1,0:T(8,128)(2,1)S(1)}, u32[]{:S(2)}, u32[]{:S(2)}) %collective-permute-start.4) | collective-permute-done | bytes 133152 | tf_op jit(solution)/shard_map/ppermute | solution.py:146
  21.4 1.4 %collective-permute-start.7 = (bf16[64,2176]{1,0:T(8,128)(2,1)S(1)}, bf16[64,2176]{1,0:T(8,128)(2,1)S(1)}, u32[]{:S(2)}, u32[]{:S(2)}) collective-permute-start(bf16[64,2176]{1,0:T(8,128)(2,1)S(1)} %get-tuple-element.22.refs_0_.refs_6_), channel_id=1, source_target_pairs={{0,1},{2,3},{1,0},{3,2},{4,5},{6,7},{5,4},{7,6},{8,9},{10,11},{9,8... | collective-permute-start | bytes 835592 | tf_op jit(solution)/shard_map/ppermute | solution.py:398
  23.5 3.9 %collective-permute-start.17 = (bf16[64,2048]{1,0:T(8,128)(2,1)S(1)}, bf16[64,2048]{1,0:T(8,128)(2,1)S(1)}, u32[]{:S(2)}, u32[]{:S(2)}) collective-permute-start(bf16[64,2048]{1,0:T(8,128)(2,1)S(1)} %get-tuple-element.25.refs_6_), channel_id=1, source_target_pairs={{0,1},{2,3},{1,0},{3,2},{4,5},{6,7},{5,4},{7,6},{8,9},{10,11},{9,8... | collective-permute-start | bytes 786440 | tf_op jit(solution)/shard_map/ppermute | solution.py:398
  28.1 1.3 collective-permute-start.12
  30.4 1.2 gather_fusion
  32.0 3.2 %collective-permute-done.17.refs_7_ = bf16[64,2048]{1,0:T(8,128)(2,1)S(1)} collective-permute-done((bf16[64,2048]{1,0:T(8,128)(2,1)S(1)}, bf16[64,2048]{1,0:T(8,128)(2,1)S(1)}, u32[]{:S(2)}, u32[]{:S(2)}) %collective-permute-start.17) | collective-permute-done | bytes 262176 | tf_op jit(solution)/shard_map/ppermute | solution.py:398
  35.3 1.4 %collective-permute-start.13 = (bf16[64,2048]{1,0:T(8,128)(2,1)S(1)}, bf16[64,2048]{1,0:T(8,128)(2,1)}, u32[]{:S(2)}, u32[]{:S(2)}) collective-permute-start(bf16[64,2048]{1,0:T(8,128)(2,1)S(1)} %get-tuple-element.23.refs_6_), channel_id=1, source_target_pairs={{1,2},{2,1},{5,6},{6,5},{9,10},{10,9},{13,14},{14,13},{17,18},{18,... | collective-permute-start | bytes 786440 | tf_op jit(solution)/shard_map/ppermute | solution.py:398
  36.7 3.1 %collective-permute-start.22 = (bf16[64,2048]{1,0:T(8,128)(2,1)S(1)}, bf16[64,2048]{1,0:T(8,128)(2,1)S(1)}, u32[]{:S(2)}, u32[]{:S(2)}) collective-permute-start(bf16[64,2048]{1,0:T(8,128)(2,1)S(1)} %get-tuple-element.31.refs_6_), channel_id=1, source_target_pairs={{0,1},{2,3},{1,0},{3,2},{4,5},{6,7},{5,4},{7,6},{8,9},{10,11},{9,8... | collective-permute-start | bytes 786440 | tf_op jit(solution)/shard_map/ppermute | solution.py:398
  39.7 1.2 collective-permute-done.12.refs_7_
  40.9 1.4 %collective-permute-start.20 = (bf16[64,2048]{1,0:T(8,128)(2,1)S(1)}, bf16[64,2048]{1,0:T(8,128)(2,1)}, u32[]{:S(2)}, u32[]{:S(2)}) collective-permute-start(bf16[64,2048]{1,0:T(8,128)(2,1)S(1)} %collective-permute-done.17.refs_7_), channel_id=1, source_target_pairs={{1,2},{2,1},{5,6},{6,5},{9,10},{10,9},{13,14},{14,13},{17,18},{18,... | collective-permute-start | bytes 786440 | tf_op jit(solution)/shard_map/ppermute | solution.py:398
  42.3 1.3 collective-permute-start.9
  43.6 1.3 collective-permute-start.11
  44.9 1.5 %fusion = pred[8]{0:T(512)(128)(4,1)S(1)} fusion(s32[8,256]{1,0:T(8,128)} %gather_fusion, s32[]{:T(128)} %bitcast.17), kind=kLoop, calls=%fused_computation.3 | loop fusion | flops 8 | bytes 44 | tf_op jit(solution)/shard_map/ge | solution.py:453
  47.6 2.2 %copy-done = bf16[256,8192]{1,0:T(8,128)(2,1)S(1)} copy-done((bf16[256,8192]{1,0:T(8,128)(2,1)S(1)}, bf16[256,8192]{1,0:T(8,128)(2,1)}, u32[]{:S(2)}) %copy-start) | copy-done | bytes 4194328
  49.8 1.2 text_scale.1.refs_13_
  51.0 0.8 collective-permute-start.23
  51.8 1.3 collective-permute-start.19
  53.2 0.7 collective-permute-start.15
  54.5 3.3 %collective-permute-done.11.refs_5_.refs_11_ = bf16[64,2176]{1,0:T(8,128)(2,1)S(1)} collective-permute-done((bf16[64,2176]{1,0:T(8,128)(2,1)S(1)}, bf16[64,2176]{1,0:T(8,128)(2,1)S(1)}, u32[]{:S(2)}, u32[]{:S(2)}) %collective-permute-start.11) | collective-permute-done | bytes 278560 | tf_op jit(solution)/shard_map/ppermute | solution.py:398
  57.8 1.3 collective-permute-start.21
  59.1 3.5 %merge_rows.4 = (bf16[256,2048]{1,0:T(8,128)(2,1)S(1)}, f32[256,512]{1,0:T(8,128)S(1)}) custom-call(bf16[64,2176]{1,0:T(8,128)(2,1)S(1)} %get-tuple-element.22.refs_0_.refs_6_, bf16[64,2176]{1,0:T(8,128)(2,1)S(1)} %collective-permute-done.7.refs_1_.refs_7_, bf16[64,2176]{1,0:T(8,128)(2,1)S(1)} %collective-permute-done.8.refs_2_.refs_8_, ...), custom_call_target="tpu_custom_call" | custom-call | flops 939524096 | bytes 5767168 | tf_op jit(solution)/shard_map/merge_rows/pallas_call | solution.py:210
  62.7 5.6 %queries.3.refs_2_ = f32[256,2048]{1,0:T(8,128)S(1)} custom-call(bf16[256,2048]{1,0:T(8,128)(2,1)S(1)} %get-tuple-element.29.refs_0_, bf16[8192,2048]{1,0:T(8,128)(2,1)} %refs_2_.1, f32[1,2048]{1,0:T(1,128)S(1)} %bitcast.29), custom_call_target="tpu_custom_call" | custom-call | flops 2147483648 | bytes 9437184 | tf_op jit(solution)/shard_map/queries/pallas_call | solution.py:271
  68.3 1.3 collective-permute-start.14
  69.6 1.3 collective-permute-start.24
  70.9 1.3 collective-permute-start.16
  72.2 1.3 collective-permute-start.26
  73.6 3.4 %merge_rows.5 = (bf16[256,2048]{1,0:T(8,128)(2,1)S(1)}, f32[256,512]{1,0:T(8,128)S(1)}) custom-call(bf16[64,2176]{1,0:T(8,128)(2,1)S(1)} %get-tuple-element.22.refs_0_.refs_6_, bf16[64,2176]{1,0:T(8,128)(2,1)S(1)} %collective-permute-done.7.refs_1_.refs_7_, bf16[64,2176]{1,0:T(8,128)(2,1)S(1)} %collective-permute-done.8.refs_2_.refs_8_, ...), custom_call_target="tpu_custom_call" | custom-call | flops 939524096 | bytes 5767168 | tf_op jit(solution)/shard_map/merge_rows/pallas_call | solution.py:210
  77.0 5.6 %queries.4.refs_18_.refs_3_ = f32[256,2048]{1,0:T(8,128)S(1)} custom-call(bf16[256,2048]{1,0:T(8,128)(2,1)S(1)} %get-tuple-element.28.refs_0_, bf16[8192,2048]{1,0:T(8,128)(2,1)} %refs_2_.1, f32[256,2048]{1,0:T(8,128)S(1)} %queries.3.refs_2_), custom_call_target="tpu_custom_call" | custom-call | flops 2147483648 | bytes 9437184 | tf_op jit(solution)/shard_map/queries/pallas_call | solution.py:271
  82.6 1.3 copy-done.1
  84.0 7.4 %collective-permute-done.16.refs_11_ = bf16[64,2048]{1,0:T(8,128)(2,1)S(1)} collective-permute-done((bf16[64,2048]{1,0:T(8,128)(2,1)S(1)}, bf16[64,2048]{1,0:T(8,128)(2,1)S(1)}, u32[]{:S(2)}, u32[]{:S(2)}) %collective-permute-start.16) | collective-permute-done | bytes 262176 | tf_op jit(solution)/shard_map/ppermute | solution.py:398
  91.4 3.3 %merge_rows.6 = (bf16[256,2048]{1,0:T(8,128)(2,1)S(1)}, f32[256,512]{1,0:T(8,128)S(1)}) custom-call(bf16[64,2176]{1,0:T(8,128)(2,1)S(1)} %get-tuple-element.22.refs_0_.refs_6_, bf16[64,2176]{1,0:T(8,128)(2,1)S(1)} %collective-permute-done.7.refs_1_.refs_7_, bf16[64,2176]{1,0:T(8,128)(2,1)S(1)} %collective-permute-done.8.refs_2_.refs_8_, ...), custom_call_target="tpu_custom_call" | custom-call | flops 939524096 | bytes 5767168 | tf_op jit(solution)/shard_map/merge_rows/pallas_call | solution.py:210
  94.7 2.3 %collective-permute-done.26.refs_11_ = bf16[64,2048]{1,0:T(8,128)(2,1)S(1)} collective-permute-done((bf16[64,2048]{1,0:T(8,128)(2,1)S(1)}, bf16[64,2048]{1,0:T(8,128)(2,1)S(1)}, u32[]{:S(2)}, u32[]{:S(2)}) %collective-permute-start.26) | collective-permute-done | bytes 262176 | tf_op jit(solution)/shard_map/ppermute | solution.py:398
  97.0 3.5 %merge_rows.7 = (bf16[256,2048]{1,0:T(8,128)(2,1)S(1)}, bf16[256,512]{1,0:T(8,128)(2,1)S(1)}) custom-call(bf16[64,2176]{1,0:T(8,128)(2,1)S(1)} %get-tuple-element.22.refs_0_.refs_6_, bf16[64,2176]{1,0:T(8,128)(2,1)S(1)} %collective-permute-done.7.refs_1_.refs_7_, bf16[64,2176]{1,0:T(8,128)(2,1)S(1)} %collective-permute-done.8.refs_2_.refs_8_, ...), custom_call_target="tpu_custom_call" | custom-call | flops 939524096 | bytes 5767168 | tf_op jit(solution)/shard_map/merge_rows/pallas_call | solution.py:210
  100.4 1.3 collective-permute-start.32
  101.7 1.3 collective-permute-start.30
  103.0 2.5 %collective-permute-start.28 = (bf16[256,512]{1,0:T(8,128)(2,1)S(1)}, bf16[256,512]{1,0:T(8,128)(2,1)S(1)}, u32[]{:S(2)}, u32[]{:S(2)}) collective-permute-start(bf16[256,512]{1,0:T(8,128)(2,1)S(1)} %get-tuple-element.35.refs_9_), channel_id=1, source_target_pairs={{0,8},{4,12},{16,24},{20,28},{1,9},{5,13},{17,25},{21,29},{2,10},{... | collective-permute-start | bytes 786440 | tf_op jit(solution)/shard_map/ppermute | solution.py:441
  105.6 8.8 %queries.5.refs_1_ = bf16[2,128,2048]{2,1,0:T(8,128)(2,1)S(1)} custom-call(bf16[256,2048]{1,0:T(8,128)(2,1)S(1)} %get-tuple-element.30.refs_0_, bf16[256,2048]{1,0:T(8,128)(2,1)S(1)} %get-tuple-element.33.refs_1_, bf16[8192,2048]{1,0:T(8,128)(2,1)} %refs_2_.1, f32[256,2048]{1,0:T(8,128)S(1)} %copy-done.2), custom_call_target="tpu_custom_call" | custom-call | flops 4294967296 | bytes 18874368 | tf_op jit(solution)/shard_map/queries/pallas_call | solution.py:271
  114.4 4.2 %collective-permute-start.27 = (bf16[256,512]{1,0:T(8,128)(2,1)S(1)}, bf16[256,512]{1,0:T(8,128)(2,1)S(1)}, u32[]{:S(2)}, u32[]{:S(2)}) collective-permute-start(bf16[256,512]{1,0:T(8,128)(2,1)S(1)} %get-tuple-element.35.refs_9_), channel_id=1, source_target_pairs={{0,4},{4,0},{8,12},{12,8},{16,20},{20,16},{24,28},{28,24},{1,5},{5... | collective-permute-start | bytes 786440 | tf_op jit(solution)/shard_map/ppermute | solution.py:448
  121.1 13.0 %attend_rest.1 = bf16[256,2048]{1,0:T(8,128)(2,1)} custom-call(s32[8]{0:T(128)S(1)} %and_convert_fusion.refs_0_, bf16[2,128,2048]{2,1,0:T(8,128)(2,1)S(1)} %queries.5.refs_1_, s32[1,256]{1,0:T(1,128)S(1)} %constant_dynamic-slice_fusion.1.refs_2_, s32[8,256,1]{2,1,0:T(8,128)S(1)} %copy.12.refs_3_, s32[8]{0:T(128)S(1)} %subtract_multiply_fusion.refs_4_, ...), custom_call_target="tpu_custom_call" | custom-call | flops 4294967296 | bytes 2097152 | tf_op jit(solution)/shard_map/attend_rest/pallas_call | solution.py:355
  (69 shorter events, 9.1 us)
Async XLA Ops:
  0.0 22.7 %copy-start.10 = (s32[2048]{0:T(1024)S(1)}, s32[2048]{0:T(1024)}, u32[]{:S(2)}) copy-start(s32[2048]{0:T(1024)} %param.15) | copy-start | bytes 24580
  0.7 1.2 copy-start.3
  2.0 0.8 copy-start.4
  2.7 0.7 copy-start.8
  4.9 54.2 %copy-start.5 = (f32[8192]{0:T(1024)S(1)}, f32[8192]{0:T(1024)}, u32[]{:S(2)}) copy-start(f32[8192]{0:T(1024)} %param.16) | copy-start | bytes 98308
  5.0 4.3 %collective-permute-start = (bf16[8,8320]{1,0:T(8,128)(2,1)S(1)}, bf16[8,8320]{1,0:T(8,128)(2,1)S(1)}, u32[]{:S(2)}, u32[]{:S(2)}) collective-permute-start(bf16[8,8320]{1,0:T(8,128)(2,1)S(1)} %get-tuple-element.45), channel_id=1, source_target_pairs={{0,4},{4,0},{8,12},{12,8},{16,20},{20,16},{24,28},{28,24},{1,5},{5... | collective-permute-start | bytes 399368 | tf_op jit(solution)/shard_map/ppermute | solution.py:146
  5.7 5.1 %collective-permute-start.1 = (bf16[8,8320]{1,0:T(8,128)(2,1)S(1)}, bf16[8,8320]{1,0:T(8,128)(2,1)S(1)}, u32[]{:S(2)}, u32[]{:S(2)}) collective-permute-start(bf16[8,8320]{1,0:T(8,128)(2,1)S(1)} %get-tuple-element.44), channel_id=1, source_target_pairs={{0,8},{4,12},{8,0},{12,4},{16,24},{20,28},{24,16},{28,20},{1,9},{5... | collective-permute-start | bytes 399368 | tf_op jit(solution)/shard_map/ppermute | solution.py:146
  7.0 7.7 %collective-permute-start.2 = (bf16[8,8320]{1,0:T(8,128)(2,1)S(1)}, bf16[8,8320]{1,0:T(8,128)(2,1)S(1)}, u32[]{:S(2)}, u32[]{:S(2)}) collective-permute-start(bf16[8,8320]{1,0:T(8,128)(2,1)S(1)} %get-tuple-element.43), channel_id=1, source_target_pairs={{0,12},{4,8},{8,4},{12,0},{16,28},{20,24},{24,20},{28,16},{1,13},{... | collective-permute-start | bytes 399368 | tf_op jit(solution)/shard_map/ppermute | solution.py:146
  7.5 7.2 %collective-permute-start.3 = (bf16[8,8320]{1,0:T(8,128)(2,1)S(1)}, bf16[8,8320]{1,0:T(8,128)(2,1)S(1)}, u32[]{:S(2)}, u32[]{:S(2)}) collective-permute-start(bf16[8,8320]{1,0:T(8,128)(2,1)S(1)} %get-tuple-element.42), channel_id=1, source_target_pairs={{0,16},{4,20},{8,24},{12,28},{16,0},{20,4},{24,8},{28,12},{1,17},{... | collective-permute-start | bytes 399368 | tf_op jit(solution)/shard_map/ppermute | solution.py:146
  7.5 13.8 %collective-permute-start.4 = (bf16[8,8320]{1,0:T(8,128)(2,1)S(1)}, bf16[8,8320]{1,0:T(8,128)(2,1)S(1)}, u32[]{:S(2)}, u32[]{:S(2)}) collective-permute-start(bf16[8,8320]{1,0:T(8,128)(2,1)S(1)} %get-tuple-element.41), channel_id=1, source_target_pairs={{0,20},{4,16},{8,28},{12,24},{16,4},{20,0},{24,12},{28,8},{1,21},{... | collective-permute-start | bytes 399368 | tf_op jit(solution)/shard_map/ppermute | solution.py:146
  9.3 12.0 %collective-permute-start.5 = (bf16[8,8320]{1,0:T(8,128)(2,1)S(1)}, bf16[8,8320]{1,0:T(8,128)(2,1)S(1)}, u32[]{:S(2)}, u32[]{:S(2)}) collective-permute-start(bf16[8,8320]{1,0:T(8,128)(2,1)S(1)} %get-tuple-element.40), channel_id=1, source_target_pairs={{0,24},{4,28},{8,16},{12,20},{16,8},{20,12},{24,0},{28,4},{1,25},{... | collective-permute-start | bytes 399368 | tf_op jit(solution)/shard_map/ppermute | solution.py:146
  10.9 10.4 %collective-permute-start.6 = (bf16[8,8320]{1,0:T(8,128)(2,1)S(1)}, bf16[8,8320]{1,0:T(8,128)(2,1)S(1)}, u32[]{:S(2)}, u32[]{:S(2)}) collective-permute-start(bf16[8,8320]{1,0:T(8,128)(2,1)S(1)} %get-tuple-element.39), channel_id=1, source_target_pairs={{0,28},{4,24},{8,20},{12,16},{16,12},{20,8},{24,4},{28,0},{1,29},{... | collective-permute-start | bytes 399368 | tf_op jit(solution)/shard_map/ppermute | solution.py:146
  21.4 8.3 %collective-permute-start.7 = (bf16[64,2176]{1,0:T(8,128)(2,1)S(1)}, bf16[64,2176]{1,0:T(8,128)(2,1)S(1)}, u32[]{:S(2)}, u32[]{:S(2)}) collective-permute-start(bf16[64,2176]{1,0:T(8,128)(2,1)S(1)} %get-tuple-element.22.refs_0_.refs_6_), channel_id=1, source_target_pairs={{0,1},{2,3},{1,0},{3,2},{4,5},{6,7},{5,4},{7,6},{8,9},{10,11},{9,8... | collective-permute-start | bytes 835592 | tf_op jit(solution)/shard_map/ppermute | solution.py:398
  22.8 19.4 %collective-permute-start.8 = (bf16[64,2176]{1,0:T(8,128)(2,1)S(1)}, bf16[64,2176]{1,0:T(8,128)(2,1)S(1)}, u32[]{:S(2)}, u32[]{:S(2)}) collective-permute-start(bf16[64,2176]{1,0:T(8,128)(2,1)S(1)} %get-tuple-element.22.refs_0_.refs_6_), channel_id=1, source_target_pairs={{1,2},{2,1},{5,6},{6,5},{9,10},{10,9},{13,14},{14,13},{17,18},{18,... | collective-permute-start | bytes 835592 | tf_op jit(solution)/shard_map/ppermute | solution.py:398
  23.5 11.8 %collective-permute-start.17 = (bf16[64,2048]{1,0:T(8,128)(2,1)S(1)}, bf16[64,2048]{1,0:T(8,128)(2,1)S(1)}, u32[]{:S(2)}, u32[]{:S(2)}) collective-permute-start(bf16[64,2048]{1,0:T(8,128)(2,1)S(1)} %get-tuple-element.25.refs_6_), channel_id=1, source_target_pairs={{0,1},{2,3},{1,0},{3,2},{4,5},{6,7},{5,4},{7,6},{8,9},{10,11},{9,8... | collective-permute-start | bytes 786440 | tf_op jit(solution)/shard_map/ppermute | solution.py:398
  27.4 9.3 %collective-permute-start.18 = (bf16[64,2048]{1,0:T(8,128)(2,1)S(1)}, bf16[64,2048]{1,0:T(8,128)(2,1)S(1)}, u32[]{:S(2)}, u32[]{:S(2)}) collective-permute-start(bf16[64,2048]{1,0:T(8,128)(2,1)S(1)} %get-tuple-element.25.refs_6_), channel_id=1, source_target_pairs={{1,2},{2,1},{5,6},{6,5},{9,10},{10,9},{13,14},{14,13},{17,18},{18,... | collective-permute-start | bytes 786440 | tf_op jit(solution)/shard_map/ppermute | solution.py:398
  28.1 12.8 %collective-permute-start.12 = (bf16[64,2048]{1,0:T(8,128)(2,1)S(1)}, bf16[64,2048]{1,0:T(8,128)(2,1)S(1)}, u32[]{:S(2)}, u32[]{:S(2)}) collective-permute-start(bf16[64,2048]{1,0:T(8,128)(2,1)S(1)} %get-tuple-element.23.refs_6_), channel_id=1, source_target_pairs={{0,1},{2,3},{1,0},{3,2},{4,5},{6,7},{5,4},{7,6},{8,9},{10,11},{9,8... | collective-permute-start | bytes 786440 | tf_op jit(solution)/shard_map/ppermute | solution.py:398
  29.7 13.9 %collective-permute-start.10 = (bf16[64,2176]{1,0:T(8,128)(2,1)S(1)}, bf16[64,2176]{1,0:T(8,128)(2,1)S(1)}, u32[]{:S(2)}, u32[]{:S(2)}) collective-permute-start(bf16[64,2176]{1,0:T(8,128)(2,1)S(1)} %collective-permute-done.7.refs_1_.refs_7_), channel_id=1, source_target_pairs={{1,2},{2,1},{5,6},{6,5},{9,10},{10,9},{13,14},{14,13},{17,18},{18,... | collective-permute-start | bytes 835592 | tf_op jit(solution)/shard_map/ppermute | solution.py:398
  35.3 15.7 %collective-permute-start.13 = (bf16[64,2048]{1,0:T(8,128)(2,1)S(1)}, bf16[64,2048]{1,0:T(8,128)(2,1)}, u32[]{:S(2)}, u32[]{:S(2)}) collective-permute-start(bf16[64,2048]{1,0:T(8,128)(2,1)S(1)} %get-tuple-element.23.refs_6_), channel_id=1, source_target_pairs={{1,2},{2,1},{5,6},{6,5},{9,10},{10,9},{13,14},{14,13},{17,18},{18,... | collective-permute-start | bytes 786440 | tf_op jit(solution)/shard_map/ppermute | solution.py:398
  36.7 15.2 %collective-permute-start.22 = (bf16[64,2048]{1,0:T(8,128)(2,1)S(1)}, bf16[64,2048]{1,0:T(8,128)(2,1)S(1)}, u32[]{:S(2)}, u32[]{:S(2)}) collective-permute-start(bf16[64,2048]{1,0:T(8,128)(2,1)S(1)} %get-tuple-element.31.refs_6_), channel_id=1, source_target_pairs={{0,1},{2,3},{1,0},{3,2},{4,5},{6,7},{5,4},{7,6},{8,9},{10,11},{9,8... | collective-permute-start | bytes 786440 | tf_op jit(solution)/shard_map/ppermute | solution.py:398
  40.9 12.3 %collective-permute-start.20 = (bf16[64,2048]{1,0:T(8,128)(2,1)S(1)}, bf16[64,2048]{1,0:T(8,128)(2,1)}, u32[]{:S(2)}, u32[]{:S(2)}) collective-permute-start(bf16[64,2048]{1,0:T(8,128)(2,1)S(1)} %collective-permute-done.17.refs_7_), channel_id=1, source_target_pairs={{1,2},{2,1},{5,6},{6,5},{9,10},{10,9},{13,14},{14,13},{17,18},{18,... | collective-permute-start | bytes 786440 | tf_op jit(solution)/shard_map/ppermute | solution.py:398
  42.3 11.6 %collective-permute-start.9 = (bf16[64,2176]{1,0:T(8,128)(2,1)S(1)}, bf16[64,2176]{1,0:T(8,128)(2,1)S(1)}, u32[]{:S(2)}, u32[]{:S(2)}) collective-permute-start(bf16[64,2176]{1,0:T(8,128)(2,1)S(1)} %collective-permute-done.8.refs_2_.refs_8_), channel_id=1, source_target_pairs={{2,3},{1,0},{6,7},{5,4},{10,11},{9,8},{14,15},{13,12},{18,19},{17,... | collective-permute-start | bytes 835592 | tf_op jit(solution)/shard_map/ppermute | solution.py:398
  43.6 14.3 %collective-permute-start.11 = (bf16[64,2176]{1,0:T(8,128)(2,1)S(1)}, bf16[64,2176]{1,0:T(8,128)(2,1)S(1)}, u32[]{:S(2)}, u32[]{:S(2)}) collective-permute-start(bf16[64,2176]{1,0:T(8,128)(2,1)S(1)} %collective-permute-done.10.refs_4_.refs_10_), channel_id=1, source_target_pairs={{2,3},{1,0},{6,7},{5,4},{10,11},{9,8},{14,15},{13,12},{18,19},{17,... | collective-permute-start | bytes 835592 | tf_op jit(solution)/shard_map/ppermute | solution.py:398
  47.6 2.2 %copy-start = (bf16[256,8192]{1,0:T(8,128)(2,1)S(1)}, bf16[256,8192]{1,0:T(8,128)(2,1)}, u32[]{:S(2)}) copy-start(bf16[256,8192]{1,0:T(8,128)(2,1)} %refs_12_.7) | copy-start | bytes 12582916
  51.0 11.7 %copy-start.6 = (f32[2048]{0:T(1024)S(1)}, f32[2048]{0:T(1024)}, u32[]{:S(2)}) copy-start(f32[2048]{0:T(1024)} %param.18) | copy-start | bytes 24580
  51.0 17.3 %collective-permute-start.23 = (bf16[64,2048]{1,0:T(8,128)(2,1)S(1)}, bf16[64,2048]{1,0:T(8,128)(2,1)S(1)}, u32[]{:S(2)}, u32[]{:S(2)}) collective-permute-start(bf16[64,2048]{1,0:T(8,128)(2,1)S(1)} %get-tuple-element.31.refs_6_), channel_id=1, source_target_pairs={{1,2},{2,1},{5,6},{6,5},{9,10},{10,9},{13,14},{14,13},{17,18},{18,... | collective-permute-start | bytes 786440 | tf_op jit(solution)/shard_map/ppermute | solution.py:398
  51.8 17.8 %collective-permute-start.19 = (bf16[64,2048]{1,0:T(8,128)(2,1)S(1)}, bf16[64,2048]{1,0:T(8,128)(2,1)S(1)}, u32[]{:S(2)}, u32[]{:S(2)}) collective-permute-start(bf16[64,2048]{1,0:T(8,128)(2,1)S(1)} %collective-permute-done.18.refs_8_), channel_id=1, source_target_pairs={{2,3},{1,0},{6,7},{5,4},{10,11},{9,8},{14,15},{13,12},{18,19},{17,... | collective-permute-start | bytes 786440 | tf_op jit(solution)/shard_map/ppermute | solution.py:398
  53.2 17.8 %collective-permute-start.15 = (bf16[64,2048]{1,0:T(8,128)(2,1)S(1)}, bf16[64,2048]{1,0:T(8,128)(2,1)S(1)}, u32[]{:S(2)}, u32[]{:S(2)}) collective-permute-start(bf16[64,2048]{1,0:T(8,128)(2,1)S(1)} %collective-permute-done.12.refs_7_), channel_id=1, source_target_pairs={{1,2},{2,1},{5,6},{6,5},{9,10},{10,9},{13,14},{14,13},{17,18},{18,... | collective-permute-start | bytes 786440 | tf_op jit(solution)/shard_map/ppermute | solution.py:398
  53.9 18.4 %collective-permute-start.25 = (bf16[64,2048]{1,0:T(8,128)(2,1)S(1)}, bf16[64,2048]{1,0:T(8,128)(2,1)S(1)}, u32[]{:S(2)}, u32[]{:S(2)}) collective-permute-start(bf16[64,2048]{1,0:T(8,128)(2,1)S(1)} %collective-permute-done.22.refs_7_), channel_id=1, source_target_pairs={{1,2},{2,1},{5,6},{6,5},{9,10},{10,9},{13,14},{14,13},{17,18},{18,... | collective-permute-start | bytes 786440 | tf_op jit(solution)/shard_map/ppermute | solution.py:398
  57.8 15.7 %collective-permute-start.21 = (bf16[64,2048]{1,0:T(8,128)(2,1)}, bf16[64,2048]{1,0:T(8,128)(2,1)S(1)}, u32[]{:S(2)}, u32[]{:S(2)}) collective-permute-start(bf16[64,2048]{1,0:T(8,128)(2,1)} %collective-permute-done.20.refs_10_), channel_id=1, source_target_pairs={{2,3},{1,0},{6,7},{5,4},{10,11},{9,8},{14,15},{13,12},{18,19},{17,... | collective-permute-start | bytes 786440 | tf_op jit(solution)/shard_map/ppermute | solution.py:398
  68.3 15.6 %collective-permute-start.14 = (bf16[64,2048]{1,0:T(8,128)(2,1)}, bf16[64,2048]{1,0:T(8,128)(2,1)S(1)}, u32[]{:S(2)}, u32[]{:S(2)}) collective-permute-start(bf16[64,2048]{1,0:T(8,128)(2,1)} %collective-permute-done.13.refs_8_), channel_id=1, source_target_pairs={{2,3},{1,0},{6,7},{5,4},{10,11},{9,8},{14,15},{13,12},{18,19},{17,... | collective-permute-start | bytes 786440 | tf_op jit(solution)/shard_map/ppermute | solution.py:398
  69.6 25.1 %collective-permute-start.24 = (bf16[64,2048]{1,0:T(8,128)(2,1)S(1)}, bf16[64,2048]{1,0:T(8,128)(2,1)S(1)}, u32[]{:S(2)}, u32[]{:S(2)}) collective-permute-start(bf16[64,2048]{1,0:T(8,128)(2,1)S(1)} %collective-permute-done.23.refs_8_), channel_id=1, source_target_pairs={{2,3},{1,0},{6,7},{5,4},{10,11},{9,8},{14,15},{13,12},{18,19},{17,... | collective-permute-start | bytes 786440 | tf_op jit(solution)/shard_map/ppermute | solution.py:398
  70.9 20.4 %collective-permute-start.16 = (bf16[64,2048]{1,0:T(8,128)(2,1)S(1)}, bf16[64,2048]{1,0:T(8,128)(2,1)S(1)}, u32[]{:S(2)}, u32[]{:S(2)}) collective-permute-start(bf16[64,2048]{1,0:T(8,128)(2,1)S(1)} %collective-permute-done.15.refs_10_), channel_id=1, source_target_pairs={{2,3},{1,0},{6,7},{5,4},{10,11},{9,8},{14,15},{13,12},{18,19},{17,... | collective-permute-start | bytes 786440 | tf_op jit(solution)/shard_map/ppermute | solution.py:398
  72.2 24.7 %collective-permute-start.26 = (bf16[64,2048]{1,0:T(8,128)(2,1)S(1)}, bf16[64,2048]{1,0:T(8,128)(2,1)S(1)}, u32[]{:S(2)}, u32[]{:S(2)}) collective-permute-start(bf16[64,2048]{1,0:T(8,128)(2,1)S(1)} %collective-permute-done.25.refs_10_), channel_id=1, source_target_pairs={{2,3},{1,0},{6,7},{5,4},{10,11},{9,8},{14,15},{13,12},{18,19},{17,... | collective-permute-start | bytes 786440 | tf_op jit(solution)/shard_map/ppermute | solution.py:398
  82.6 1.3 copy-start.1
  91.4 5.6 %copy-start.7 = (f32[256]{0:T(256)S(1)}, f32[256]{0:T(256)}, u32[]{:S(2)}) copy-start(f32[256]{0:T(256)} %param.21) | copy-start | bytes 3076
  97.0 8.6 %copy-start.2 = (f32[256,2048]{1,0:T(8,128)S(1)}, f32[256,2048]{1,0:T(8,128)}, u32[]{:S(2)}) copy-start(f32[256,2048]{1,0:T(8,128)} %copy-done.1) | copy-start | bytes 6291460
  100.4 18.2 %collective-permute-start.32 = (bf16[256,512]{1,0:T(8,128)(2,1)S(1)}, bf16[256,512]{1,0:T(8,128)(2,1)S(1)}, u32[]{:S(2)}, u32[]{:S(2)}) collective-permute-start(bf16[256,512]{1,0:T(8,128)(2,1)S(1)} %get-tuple-element.35.refs_9_), channel_id=1, source_target_pairs={{8,16},{12,20},{9,17},{13,21},{10,18},{14,22},{11,19},{15,23}} | collective-permute-start | bytes 786440 | tf_op jit(solution)/shard_map/ppermute | solution.py:441
  101.7 17.0 %collective-permute-start.30 = (bf16[256,512]{1,0:T(8,128)(2,1)S(1)}, bf16[256,512]{1,0:T(8,128)(2,1)S(1)}, u32[]{:S(2)}, u32[]{:S(2)}) collective-permute-start(bf16[256,512]{1,0:T(8,128)(2,1)S(1)} %get-tuple-element.35.refs_9_), channel_id=1, source_target_pairs={{0,16},{4,20},{8,24},{12,28},{1,17},{5,21},{9,25},{13,29},{2,18},{... | collective-permute-start | bytes 786440 | tf_op jit(solution)/shard_map/ppermute | solution.py:441
  103.0 16.1 %collective-permute-start.28 = (bf16[256,512]{1,0:T(8,128)(2,1)S(1)}, bf16[256,512]{1,0:T(8,128)(2,1)S(1)}, u32[]{:S(2)}, u32[]{:S(2)}) collective-permute-start(bf16[256,512]{1,0:T(8,128)(2,1)S(1)} %get-tuple-element.35.refs_9_), channel_id=1, source_target_pairs={{0,8},{4,12},{16,24},{20,28},{1,9},{5,13},{17,25},{21,29},{2,10},{... | collective-permute-start | bytes 786440 | tf_op jit(solution)/shard_map/ppermute | solution.py:441
  105.6 13.7 %copy-start.9 = (s32[8,256]{1,0:T(8,128)S(1)}, s32[8,256]{1,0:T(8,128)}, u32[]{:S(2)}) copy-start(s32[8,256]{1,0:T(8,128)} %gather_fusion) | copy-start | bytes 24580
  105.6 14.1 %copy-start.11 = (s32[8]{0:T(128)S(1)}, s32[8]{0:T(128)}, u32[]{:S(2)}) copy-start(s32[8]{0:T(128)} %stack.57) | copy-start | bytes 100
  114.4 5.4 %collective-permute-start.27 = (bf16[256,512]{1,0:T(8,128)(2,1)S(1)}, bf16[256,512]{1,0:T(8,128)(2,1)S(1)}, u32[]{:S(2)}, u32[]{:S(2)}) collective-permute-start(bf16[256,512]{1,0:T(8,128)(2,1)S(1)} %get-tuple-element.35.refs_9_), channel_id=1, source_target_pairs={{0,4},{4,0},{8,12},{12,8},{16,20},{20,16},{24,28},{28,24},{1,5},{5... | collective-permute-start | bytes 786440 | tf_op jit(solution)/shard_map/ppermute | solution.py:448
  118.6 1.7 %collective-permute-start.33 = (bf16[256,512]{1,0:T(8,128)(2,1)S(1)}, bf16[256,512]{1,0:T(8,128)(2,1)}, u32[]{:S(2)}, u32[]{:S(2)}) collective-permute-start(bf16[256,512]{1,0:T(8,128)(2,1)S(1)} %collective-permute-done.32.refs_12_), channel_id=1, source_target_pairs={{0,4},{4,0},{8,12},{12,8},{16,20},{20,16},{24,28},{28,24},{1,5},{5... | collective-permute-start | bytes 786440 | tf_op jit(solution)/shard_map/ppermute | solution.py:448
  118.7 2.0 %collective-permute-start.31 = (bf16[256,512]{1,0:T(8,128)(2,1)S(1)}, bf16[256,512]{1,0:T(8,128)(2,1)}, u32[]{:S(2)}, u32[]{:S(2)}) collective-permute-start(bf16[256,512]{1,0:T(8,128)(2,1)S(1)} %collective-permute-done.30.refs_11_), channel_id=1, source_target_pairs={{0,4},{4,0},{8,12},{12,8},{16,20},{20,16},{24,28},{28,24},{1,5},{5... | collective-permute-start | bytes 786440 | tf_op jit(solution)/shard_map/ppermute | solution.py:448
  119.2 1.9 %collective-permute-start.29 = (bf16[256,512]{1,0:T(8,128)(2,1)S(1)}, bf16[256,512]{1,0:T(8,128)(2,1)}, u32[]{:S(2)}, u32[]{:S(2)}) collective-permute-start(bf16[256,512]{1,0:T(8,128)(2,1)S(1)} %collective-permute-done.28.refs_10_), channel_id=1, source_target_pairs={{0,4},{4,0},{8,12},{12,8},{16,20},{20,16},{24,28},{28,24},{1,5},{5... | collective-permute-start | bytes 786440 | tf_op jit(solution)/shard_map/ppermute | solution.py:448
